TPU v7x, 256 devices: a whole 4x4x8 slice. The times are simulated.
256 devices in a mesh: rep: 4 (over x), fsdp: 16 (over z, core), tp: 4 (over y).
Axes of the slice: x: 4, y: 4, z: 8, core: 2. Of those that a mesh axis runs over, the one named last changes fastest.
Arguments:
- weights: float32 [1024, 53248], P('tp', 'fsdp'), may hold values from -0.1875 to 0.1875
- momentum: float32 [4096, 53248], P(('rep', 'tp'), 'fsdp'), may hold values from -6 to 6
- gradient: float32 [4096, 53248], P(('rep', 'tp'), 'fsdp'), may hold values from -120 to 120, as said below
- right_factor: float32 [53248, 256], P('fsdp', 'tp'), may hold values from -6 to 6
Outputs:
- new_weights: float32 [1024, 53248], P('tp', 'fsdp')
- new_momentum: float32 [4096, 53248], P(('rep', 'tp'), 'fsdp')
- new_right: float32 [53248, 256], P('fsdp', 'tp')
Inputs may be any that keep to these rules, and one draw needn't show every extreme that they name: `gradient`: finite values.
All inputs are finite; a program needn't handle non-finite values.
Results may differ from a plain program's by a relative error of at most 0.0003.
Values sent between devices are 32-bit elements; how exact they have to be, the bound alone decides.
A program may use at most 128 MiB of HBM per device.

v0:
```python
import jax
import jax.numpy as jnp
from jax import lax
from jax.sharding import PartitionSpec as P

momentum_decay = 0.95
learning_rate = 0.05
norm_eps = 1e-06


def matmul(left_side, right_side):
    return jnp.dot(
        left_side, right_side, preferred_element_type=jnp.float32, precision=lax.Precision.HIGHEST
    )


def local(weights, momentum, gradient, right_factor):
    replicas = lax.axis_size("rep")
    total_cols = weights.shape[1] * lax.axis_size("fsdp")
    combined = momentum + gradient
    partial_left = matmul(combined, lax.all_gather(right_factor, "tp", axis=1, tiled=True))
    left = lax.psum(partial_left, ("rep", "fsdp"))
    left = left / replicas
    gram = lax.psum(matmul(left.T, left), "tp")
    lower = jnp.linalg.cholesky(gram)
    ortho = lax.linalg.triangular_solve(lower, left, left_side=False, lower=True, transpose_a=True)
    right_t = lax.psum(matmul(ortho.T, combined), ("rep", "tp")) / replicas
    squares = lax.psum(jnp.sum(right_t * right_t, axis=1), "fsdp")
    normal_t = right_t * lax.rsqrt(squares / total_cols + norm_eps)[:, None]
    share = normal_t.shape[0] // lax.axis_size("tp")
    start = lax.axis_index("tp") * share
    new_right = lax.dynamic_slice_in_dim(normal_t, start, share, 0).T
    new_momentum = combined - (1.0 - momentum_decay) * matmul(ortho, right_t)
    new_weights = weights - learning_rate * matmul(ortho, normal_t)
    return (new_weights, new_momentum, new_right)


def solution(mesh):
    return jax.shard_map(
        local,
        mesh=mesh,
        in_specs=(
            P("tp", "fsdp"),
            P(("rep", "tp"), "fsdp"),
            P(("rep", "tp"), "fsdp"),
            P("fsdp", "tp"),
        ),
        out_specs=(P("tp", "fsdp"), P(("rep", "tp"), "fsdp"), P("fsdp", "tp")),
        check_vma=False,
    )
```

profile of v0, /device:TPU:1, one launch (start us, length us, event | category | flops | bytes accessed | tf_op | source)
XLA Modules:
  0.0 523.9 jit_solution(8677836410978888497)
XLA Ops:
  7.2 0.0 all-gather.2.cloned.1.call-start
  7.2 0.7 all-gather.2.cloned.1.call-update
  7.9 0.0 all-reduce.5.cloned.1.call-start
  7.9 3.3 add.42
  11.3 46.7 %all-gather.2.cloned.1.call-done = f32[3328,256]{0,1:T(8,128)} async-done(((f32[3328,64]{0,1:T(8,128)}), f32[3328,256]{0,1:T(8,128)}) %all-gather.2.cloned.1.call-update) | async-done | bytes 3407888 | tf_op jit(solution)/shard_map/all_gather | solution.py:21
  58.0 5.6 %fusion.19 = f32[256,256]{1,0:T(8,128)} fusion(f32[256,3328]{1,0:T(8,128)S(1)} %add.42, f32[3328,256]{0,1:T(8,128)} %all-gather.2.cloned.1.call-done), kind=kOutput, calls=%fused_computation.46 | convolution fusion | flops 2617245696 | bytes 7077888 | tf_op jit(solution)/shard_map/dot_general | solution.py:12
  63.5 0.0 all-reduce.5.cloned.1.call-update
  63.6 0.0 all-reduce.7.cloned.1.call-start
  63.6 175.6 %all-reduce.5.cloned.1.call-done = f32[256,256]{1,0:T(8,128)} async-done(((f32[256,256]{1,0:T(8,128)}), f32[256,256]{1,0:T(8,128)}) %all-reduce.5.cloned.1.call-update) | async-done | bytes 262160 | tf_op jit(solution)/shard_map/psum | solution.py:22
  239.2 2.3 fusion.17
  241.5 0.0 all-reduce.7.cloned.1.call-update
  241.6 0.2 all-reduce.9.cloned.1.call-start
  241.8 1.7 broadcast_multiply_fusion.1
  243.5 40.6 %all-reduce.7.cloned.1.call-done = f32[256,256]{0,1:T(8,128)} async-done(((f32[256,256]{0,1:T(8,128)}), f32[256,256]{0,1:T(8,128)}) %all-reduce.7.cloned.1.call-update) | async-done | bytes 262160 | tf_op jit(solution)/shard_map/psum | solution.py:24
  284.1 1.8 copy.8
  285.9 1.1 fusion.4
  287.0 0.0 copy-start.4
  287.0 0.7 copy-done.4
  287.7 11.7 %cholesky.50 = f32[128,128]{1,0:T(8,128)S(1)} custom-call(f32[128,128]{1,0:T(8,128)S(1)} %cholesky.118), custom_call_target="Cholesky" | custom-call | tf_op jit(solution)/shard_map/jit(cholesky)/cholesky | solution.py:25
  299.4 10.4 %custom-call.14 = f32[1,128,128]{1,2,0:T(8,128)} custom-call(f32[1,128,128]{2,1,0:T(8,128)S(1)} %get-tuple-element.24), custom_call_target="InvertDiagBlocksLowerTriangular" | custom-call | tf_op jit(solution)/shard_map/jit(cholesky)/cholesky | solution.py:25
  309.9 0.7 cholesky.113
  310.6 1.7 constant_dynamic-update-slice_fusion
  312.3 1.1 convolution_subtract_fusion.1
  313.4 11.7 %cholesky.105 = f32[128,128]{1,0:T(8,128)S(1)} custom-call(f32[128,128]{1,0:T(8,128)S(1)} %convolution_subtract_fusion.1), custom_call_target="Cholesky" | custom-call | tf_op jit(solution)/shard_map/jit(cholesky)/cholesky | solution.py:25
  325.1 0.6 select_reduce_fusion
  325.8 0.7 compare_reduce_fusion
  327.8 1.7 select_select_fusion
  329.5 0.1 triangular_solve.58
  329.6 7.1 %while.1 = (s32[]{:T(128)}, f32[256,256]{1,0:T(8,128)}, s32[2,2]{1,0:T(2,128)S(1)}, f32[2,128,128]{2,1,0:T(8,128)}, s32[]{:T(128)}) while((s32[]{:T(128)}, f32[256,256]{1,0:T(8,128)}, s32[2,2]{1,0:T(2,128)S(1)}, f32[2,128,128]{2,1,0:T(8,128)}, s32[]{:T(128)}) %tuple.27), condition=%wide.while_cond, body=%wide.while_body.sunk | while | flops 2 | bytes 132705 | solution.py:26
  329.6 0.6 fusion.29
  330.2 3.0 bitcast_dynamic-update-slice_fusion.2
  333.1 0.6 fusion.29
  333.7 2.9 bitcast_dynamic-update-slice_fusion.2
  336.6 21.1 %custom-call.15 = f32[2,128,128]{1,2,0:T(8,128)} custom-call(f32[2,128,128]{2,1,0:T(8,128)} %get-tuple-element.10), custom_call_target="InvertDiagBlocksLowerTriangular" | custom-call | tf_op jit(solution)/shard_map/triangular_solve | solution.py:26
  357.7 1.2 fusion.6
  359.0 1.3 convolution_subtract_fusion
  360.3 1.2 fusion.8
  361.5 0.6 copy-done.2
  362.1 4.8 fusion.5
  366.9 0.0 all-reduce.9.cloned.1.call-update
  366.9 109.6 %all-reduce.9.cloned.1.call-done = f32[256,3328]{1,0:T(8,128)} async-done(((f32[256,3328]{1,0:T(8,128)}), f32[256,3328]{1,0:T(8,128)}) %all-reduce.9.cloned.1.call-update) | async-done | bytes 3407888 | tf_op jit(solution)/shard_map/psum | solution.py:27
  476.6 2.4 multiply_reduce_fusion
  479.0 24.4 %psum.31 = f32[256]{0:T(256)S(1)} all-reduce(f32[256]{0:T(256)S(1)} %multiply_reduce_fusion), channel_id=1, replica_groups=mesh['rep'=4,'fsdp'=16,'tp'=4] {'fsdp'}, use_global_device_ids=true, to_apply=%region_8.9 | all-reduce | flops 256 | bytes 2048 | tf_op jit(solution)/shard_map/psum | solution.py:28
  503.4 2.4 broadcast_multiply_fusion
  505.8 0.6 copy-done.1
  506.4 5.2 fusion.1
  511.5 1.0 dynamic-slice_bitcast_fusion
  512.5 4.9 fusion
  (13 shorter events, 0.1 us)
Async XLA Ops:
  7.2 50.8 %all-gather.2.cloned.1.call-start = ((), (), s32[]{:S(2)}) async-start(), calls=%async_computation | async-start | bytes 4259840 | tf_op jit(solution)/shard_map/all_gather | solution.py:21
  7.9 231.3 %all-reduce.5.cloned.1.call-start = ((), (), s32[]{:S(2)}) async-start(), calls=%async_computation.1 | async-start | bytes 524288 | tf_op jit(solution)/shard_map/psum | solution.py:22
  63.6 220.6 %all-reduce.7.cloned.1.call-start = ((), (), s32[]{:S(2)}) async-start(), calls=%async_computation.2 | async-start | bytes 524288 | tf_op jit(solution)/shard_map/psum | solution.py:24
  241.6 235.0 %all-reduce.9.cloned.1.call-start = ((), (), s32[]{:S(2)}) async-start(), calls=%async_computation.3 | async-start | bytes 6815744 | tf_op jit(solution)/shard_map/psum | solution.py:27
  287.0 0.7 copy-start.4
  361.5 0.7 copy-start.2
  503.4 3.0 copy-start.1
  503.4 3.0 copy-start.3
  506.4 6.1 %copy-start = (f32[256,3328]{1,0:T(8,128)S(1)}, f32[256,3328]{1,0:T(8,128)}, u32[]{:S(2)}) copy-start(f32[256,3328]{1,0:T(8,128)} %all-reduce.9.cloned.1.call-done) | copy-start | bytes 10223620
Sparse Core Ops, SparseCore 0:
  9.8 48.0 all-gather.1
  63.7 175.4 all-reduce.4
  242.2 41.8 all-reduce.6
  367.1 109.4 all-reduce.8
where the time goes:
time: 525 us; the launch traced here: 524 us
  waiting for transfers between devices  373 us (71%)
  other arithmetic  68.9 us (13%)
  matrix products  29.3 us (6%)
  blocking collectives  24.4 us (5%)
  between operations  15.2 us (3%)
  local copies, waits for them, and re-layouts  12.5 us (2%)
    psum x1, waiting for transfers between devices, local(): left = lax.psum(partial_left, ('rep', 'fsdp'))  176 us
    psum x1, waiting for transfers between devices, local(): right_t = lax.psum(matmul(ortho.T, combined), ('rep', 'tp')) / replicas  110 us
    all_gather x1, waiting for transfers between devices, local(): lax.all_gather(right_factor, 'tp', axis=1, tiled=True)  46.7 us
    psum x1, waiting for transfers between devices, local(): gram = lax.psum(matmul(left.T, left), 'tp')  40.6 us
    another operation x6, other arithmetic, local(): lower = jnp.linalg.cholesky(gram)  35.3 us
    psum x1, blocking collectives, local(): squares = lax.psum(jnp.sum(right_t * right_t, axis=1), 'fsdp')  24.4 us
    another operation x3, other arithmetic, local(): lax.linalg.triangular_solve(lower, left, left_side=False, lower=True, tra...  22.8 us
    dot_general x5, matrix products, matmul(): jnp.dot(left_side, right_side, preferred_element_type=jnp.float32, precis...  22.8 us
  transfers between devices with their start and end apart: 4, of which 4 were waited for; matrix products, arithmetic and copies ran while one was open for 1% of the time, Pallas kernels for 0%

commit v1 on v0

v1 whole, which is shorter than its diff:
```python
import jax
import jax.numpy as jnp
from jax import lax
from jax.experimental import pallas as pl
from jax.experimental.pallas import tpu as pltpu
from jax.sharding import PartitionSpec as P

MESH = pl.DeviceIdType.MESH
HIGHEST = lax.Precision.HIGHEST
F32 = jnp.float32
BF16 = jnp.bfloat16

momentum_decay = 0.95
learning_rate = 0.05
norm_eps = 1e-06

ROWS = 256
COLS = 3328
CHUNK = 832
EARLY = 512
LATE = CHUNK - EARLY
TOTAL_COLS = 53248
NB = 64
STEP = 8


def dot(a, b, dims=((1,), (0,)), precision=None):
    return lax.dot_general(a, b, (dims, ((), ())), precision=precision, preferred_element_type=F32)


def split(a):
    high = a.astype(BF16)
    return high, (a - high.astype(F32)).astype(BF16)


def dot3(a, b, dims=((1,), (0,))):
    ah, al = split(a)
    bh, bl = split(b)
    return dot(ah, bh, dims) + (dot(ah, bl, dims) + dot(al, bh, dims))


def small_inverse(d):
    rows = lax.broadcasted_iota(jnp.int32, (NB, 128), 0)
    cols = lax.broadcasted_iota(jnp.int32, (NB, 128), 1)
    eye = jnp.where(cols == rows + 64, 1.0, 0.0).astype(F32)
    x = jnp.concatenate([d, jnp.zeros((NB, 128 - NB), F32)], axis=1) + eye
    pivots = jnp.zeros((NB, 128), F32)
    for j in range(0, NB, STEP):
        c = [jnp.broadcast_to(x[:, j + b : j + b + 1], (NB, 128)) for b in range(STEP)]
        r = [x[j + a : j + a + 1, :] for a in range(STEP)]
        update = None
        for b in range(STEP):
            pivot = c[b][j + b : j + b + 1, :]
            pivots = jnp.where(rows == j + b, pivot, pivots)
            factor = jnp.where(rows > j + b, c[b] * (1.0 / pivot), 0.0)
            for later in range(b + 1, STEP):
                c[later] = c[later] - factor * c[later][j + b : j + b + 1, :]
                r[later] = r[later] - factor[j + later : j + later + 1, :] * r[b]
            term = factor * r[b]
            update = term if update is None else update + term
        x = x - update
    x = x * lax.rsqrt(pivots)
    return x[:, 64 : 64 + NB]


def cholesky_step(m_ref, b):
    n = ROWS
    m = m_ref[...]
    w = small_inverse(m[0:NB, 0:NB])
    col = lax.broadcasted_iota(jnp.int32, (n, n), 1)
    top = dot(w, m[0:NB, :], precision=HIGHEST)
    top = jnp.concatenate([w, top[:, NB:]], axis=1)
    below = dot(m[:, 0:NB], w, ((1,), (1,)), HIGHEST)
    row = lax.broadcasted_iota(jnp.int32, (n, NB), 0)
    below = jnp.where((row >= NB) & (row < n - NB * b), below, 0.0)
    new = jnp.where(col < NB, 0.0, m) - dot(below, top, precision=HIGHEST)
    new = jnp.concatenate([new[NB:], top], axis=0)
    m_ref[...] = jnp.concatenate([new[:, NB:], new[:, :NB]], axis=1)


class Links:
    def __init__(self, send, recv):
        self.send, self.recv, self.used, self.copies = send, recv, 0, []

    def start(self, src, dst, device):
        copy = pltpu.make_async_remote_copy(
            src_ref=src,
            dst_ref=dst,
            send_sem=self.send.at[self.used],
            recv_sem=self.recv.at[self.used],
            device_id=device,
            device_id_type=MESH,
        )
        copy.start()
        self.used += 1
        self.copies.append(copy)
        return copy

    def drain(self):
        for copy in self.copies:
            copy.wait_send()


class RingSum:
    def __init__(self, links, me, to, part, relay, landing):
        self.links, self.me, self.to, self.part = links, me, to, part
        self.relay, self.landing = relay, landing
        self.right, self.left, self.far = (lax.rem(me + d, 4) for d in (1, 3, 2))

    def start(self):
        go = self.links.start
        right, left = self.to(self.right), self.to(self.left)
        self.a = go(self.part(self.far, 0), self.relay.at[0], right)
        self.b = go(self.part(self.far, 1), self.relay.at[1], left)
        self.c = go(self.part(self.right, 1), self.landing.at[0, 1], right)
        self.d = go(self.part(self.left, 0), self.landing.at[1, 0], left)

    def middle(self):
        go = self.links.start
        self.a.wait_recv()
        self.relay[0] = self.relay[0] + self.part(self.right, 0)[...]
        self.e = go(self.relay.at[0], self.landing.at[0, 0], self.to(self.right))
        self.b.wait_recv()
        self.relay[1] = self.relay[1] + self.part(self.left, 1)[...]
        self.f = go(self.relay.at[1], self.landing.at[1, 1], self.to(self.left))

    def finish(self, half):
        for copy in (self.d, self.e) if half == 0 else (self.c, self.f):
            copy.wait_recv()
        return self.part(self.me, half)[...] + (self.landing[0, half] + self.landing[1, half])


class RingGather:
    def __init__(self, links, me, to, part):
        self.links, self.me, self.to, self.part = links, me, to, part
        self.right, self.left = lax.rem(me + 1, 4), lax.rem(me + 3, 4)

    def go(self, place, half, device):
        ref = self.part(place, half)
        return self.links.start(ref, ref, self.to(device))

    def start(self):
        self.a = self.go(self.me, 0, self.right)
        self.b = self.go(self.me, 1, self.left)
        self.c = self.go(self.me, 1, self.right)
        self.d = self.go(self.me, 0, self.left)

    def middle(self):
        self.a.wait_recv()
        self.e = self.go(self.left, 0, self.right)
        self.b.wait_recv()
        self.f = self.go(self.right, 1, self.left)

    def near(self):
        self.c.wait_recv()
        self.d.wait_recv()

    def finish(self):
        self.near()
        self.e.wait_recv()
        self.f.wait_recv()


def exchange_kernel(
    momentum, gradient, right_in, right_out, ortho_out, scale_out,
    mom, grad, rown, comb, rall, summed, relay_b, landing_b, relay_a, landing_a,
    part_left, core_in, tiles, tiles_in, tile_out, left_tiles, left_t,
    gram_y, gram_all, chol, part_t, relay_t, landing_t, t_all, squares,
    send, recv, load, many,
):
    x, f, y = lax.axis_index("rep"), lax.axis_index("fsdp"), lax.axis_index("tp")
    z, core = f // 2, lax.rem(f, 2)
    q = x * 8 + z

    def at(x=x, z=z, core=core, y=y):
        return {"rep": x, "fsdp": z * 2 + core, "tp": y}

    def plane(d):
        other = lax.rem(q + d, 32)
        return other, at(x=other // 8, z=lax.rem(other, 8))

    to_x = lambda p: at(x=p)
    to_y = lambda p: at(y=p)
    partner = at(core=1 - core)
    links = Links(send, recv)

    load_r = pltpu.make_async_copy(right_in, rown, load.at[0])
    load_m = pltpu.make_async_copy(momentum, mom, load.at[1])
    load_g = pltpu.make_async_copy(gradient, grad, load.at[2])
    load_r.start()
    load_m.start()
    load_g.start()

    barrier = pltpu.get_barrier_semaphore()

    def greet(d, carry):
        pl.semaphore_signal(barrier, inc=1, device_id=plane(d)[1], device_id_type=MESH)
        return carry

    for d in (1, 2, 3):
        pl.semaphore_signal(barrier, inc=1, device_id=to_y(lax.rem(y + d, 4)), device_id_type=MESH)
    pl.semaphore_signal(barrier, inc=1, device_id=partner, device_id_type=MESH)
    lax.fori_loop(1, 32, greet, 0)

    load_r.wait()
    for p in range(4):
        rall[p, pl.ds(pl.multiple_of(64 * y, 64), 64), :] = rown[:, CHUNK * p : CHUNK * (p + 1)]
    load_m.wait()
    load_g.wait()
    for p in range(4):
        cols = slice(CHUNK * p, CHUNK * (p + 1))
        comb[p] = mom[:, cols] + grad[:, cols]
    pl.semaphore_wait(barrier, 35)

    def rank_rows(p, h):
        return pl.ds(pl.multiple_of(64 * p + 32 * h, 32), 32)

    def half(h):
        return slice(128 * h, 128 * (h + 1))

    sum_b = RingSum(links, x, to_x, lambda p, h: comb.at[p, half(h), 0:EARLY], relay_b, landing_b)
    gather_b = RingGather(links, y, to_y, lambda p, h: rall.at[x, rank_rows(p, h), 0:EARLY])
    gather_a = RingGather(links, y, to_y, lambda p, h: rall.at[:, rank_rows(p, h), EARLY:CHUNK])
    sum_b.start()
    gather_b.start()
    gather_a.start()
    gather_b.middle()
    sum_b.middle()
    gather_a.middle()
    gather_b.finish()
    gather_a.finish()
    total = None
    for p in range(4):
        term = dot3(comb[p, :, EARLY:CHUNK], rall[p, :, EARLY:CHUNK], ((1,), (1,)))
        total = term if total is None else total + term
    for h in range(2):
        summed[half(h), 0:EARLY] = sum_b.finish(h)
    total = total + dot3(summed[:, 0:EARLY], rall[x, :, 0:EARLY], ((1,), (1,)))
    part_left[0] = total[0:128]
    part_left[1] = total[128:256]

    swap = links.start(part_left.at[1 - core], core_in, partner)
    sum_a = RingSum(links, x, to_x, lambda p, h: comb.at[p, half(h), EARLY:CHUNK], relay_a, landing_a)
    sum_a.start()
    swap.wait_recv()
    mine = part_left[core] + core_in[...]
    tiles[0:16] = mine[:, 0:128].reshape(16, 8, 128)
    tiles[16:32] = mine[:, 128:256].reshape(16, 8, 128)

    def scatter(d, carry):
        other, device = plane(d)
        pltpu.make_async_remote_copy(
            src_ref=tiles.at[other], dst_ref=tiles_in.at[d - 1], send_sem=many.at[0],
            recv_sem=many.at[1], device_id=device, device_id_type=MESH,
        ).start()
        return carry

    def gather(d, carry):
        pltpu.make_async_remote_copy(
            src_ref=tile_out, dst_ref=left_tiles.at[core, q], send_sem=many.at[2],
            recv_sem=many.at[3], device_id=plane(d)[1], device_id_type=MESH,
        ).start()
        return carry

    def wait_many(i, ref):
        pltpu.make_async_copy(ref, ref, many.at[i]).wait()

    lax.fori_loop(1, 32, scatter, 0)
    wait_many(1, tiles_in)
    tile = (tiles[q] + jnp.sum(tiles_in[...], axis=0)) * 0.25
    tile_out[...] = tile
    left_tiles[core, q] = tile
    lax.fori_loop(1, 32, gather, 0)
    sum_a.middle()
    wait_many(3, tiles_in)
    swap = links.start(left_tiles.at[core], left_tiles.at[core], partner)
    for h in range(2):
        summed[half(h), EARLY:CHUNK] = sum_a.finish(h)
    swap.wait_recv()
    left = jnp.concatenate(
        [
            jnp.concatenate([left_tiles[h, 0:16].reshape(128, 128), left_tiles[h, 16:32].reshape(128, 128)], axis=1)
            for h in range(2)
        ],
        axis=0,
    )
    left_t[...] = left.T

    for h in range(2):
        part_t[h] = dot3(left_t[half(h), :], summed[...])

    def y_rows(p, lo=0, n=32):
        return pl.ds(pl.multiple_of(32 * p + lo, n), n)

    sum_t = RingSum(links, y, to_y, lambda p, h: part_t.at[h, y_rows(p)], relay_t, landing_t)
    sum_t.start()
    slab = left_t[pl.ds(pl.multiple_of((core * 4 + x) * 32, 32), 32), :]
    gram_y[y] = dot(slab, left, precision=HIGHEST)
    grams = [links.start(gram_y.at[y], gram_y.at[y], to_y(lax.rem(y + d, 4))) for d in (1, 3, 2)]
    for copy in grams:
        copy.wait_recv()
    gram_all[core, x] = (gram_y[0] + gram_y[1]) + (gram_y[2] + gram_y[3])
    grams = [links.start(gram_all.at[core, x], gram_all.at[core, x], to_x(lax.rem(x + d, 4))) for d in (1, 3, 2)]
    sum_t.middle()
    for copy in grams:
        copy.wait_recv()
    swap = links.start(gram_all.at[core], gram_all.at[core], partner)
    for h in range(2):
        t_all[h, x, y_rows(y), :] = sum_t.finish(h)

    y_first = RingGather(links, y, to_y, lambda p, h: t_all.at[0, x, y_rows(p, 16 * h, 16)])
    x_first = RingGather(links, x, to_x, lambda p, h: t_all.at[1, p, y_rows(y, 16 * h, 16)])
    y_first.start()
    x_first.start()
    swap.wait_recv()
    for c in range(2):
        for p in range(4):
            chol[128 * c + 32 * p : 128 * c + 32 * p + 32, :] = gram_all[c, p]
    y_first.middle()
    x_first.middle()
    cholesky_step(chol, 0)
    y_first.finish()
    x_first.finish()
    then_x = RingGather(links, x, to_x, lambda p, h: t_all.at[0, p, slice(64 * h, 64 * (h + 1))])
    then_y = RingGather(links, y, to_y, lambda p, h: t_all.at[1, :, y_rows(p, 16 * h, 16)])
    then_x.start()
    then_y.start()
    cholesky_step(chol, 1)
    cholesky_step(chol, 2)
    then_x.middle()
    then_y.middle()
    cholesky_step(chol, 3)
    inverse = chol[...]
    ortho_out[...] = dot(left, inverse, ((1,), (1,)), HIGHEST)
    then_x.finish()
    then_y.finish()

    ih, il = split(inverse * 0.25)
    sums = None
    for p in range(4):
        th, tl = split(jnp.concatenate([t_all[0, p], t_all[1, p]], axis=0))
        right = dot(ih, th) + (dot(ih, tl) + dot(il, th))
        right_out[:, CHUNK * p : CHUNK * (p + 1)] = right
        term = jnp.sum(right * right, axis=1, keepdims=True)
        sums = term if sums is None else sums + term
    squares[f] = jnp.broadcast_to(sums, (ROWS, 128)).T[0:8]

    def share(d, carry):
        other = lax.rem(f + d, 16)
        pltpu.make_async_remote_copy(
            src_ref=squares.at[f], dst_ref=squares.at[f], send_sem=many.at[4],
            recv_sem=many.at[5], device_id=at(z=other // 2, core=lax.rem(other, 2)), device_id_type=MESH,
        ).start()
        return carry

    lax.fori_loop(1, 16, share, 0)
    wait_many(5, squares.at[0:15])
    scale_out[...] = lax.rsqrt(jnp.sum(squares[...], axis=0) / TOTAL_COLS + norm_eps)
    wait_many(0, tiles_in)
    wait_many(2, tiles_in)
    wait_many(4, squares.at[0:15])
    links.drain()


def exchange(momentum, gradient, right_t):
    vmem = lambda *shape: pltpu.VMEM(shape, F32)
    return pl.pallas_call(
        exchange_kernel,
        out_shape=(
            jax.ShapeDtypeStruct((ROWS, COLS), F32),
            jax.ShapeDtypeStruct((ROWS, ROWS), F32),
            jax.ShapeDtypeStruct((8, ROWS), F32),
        ),
        in_specs=[pl.BlockSpec(memory_space=pl.ANY)] * 3,
        out_specs=(pl.BlockSpec(memory_space=pltpu.VMEM),) * 3,
        scratch_shapes=[
            vmem(ROWS, COLS),
            vmem(ROWS, COLS),
            vmem(64, COLS),
            vmem(4, ROWS, CHUNK),
            vmem(4, ROWS, CHUNK),
            vmem(ROWS, CHUNK),
            vmem(2, 128, EARLY),
            vmem(2, 2, 128, EARLY),
            vmem(2, 128, LATE),
            vmem(2, 2, 128, LATE),
            vmem(2, 128, ROWS),
            vmem(128, ROWS),
            vmem(32, 8, 128),
            vmem(31, 8, 128),
            vmem(8, 128),
            vmem(2, 32, 8, 128),
            vmem(ROWS, ROWS),
            vmem(4, 32, ROWS),
            vmem(2, 4, 32, ROWS),
            vmem(ROWS, ROWS),
            vmem(2, 128, CHUNK),
            vmem(2, 32, CHUNK),
            vmem(2, 2, 32, CHUNK),
            vmem(2, 4, 128, CHUNK),
            vmem(16, 8, ROWS),
            pltpu.SemaphoreType.DMA((64,)),
            pltpu.SemaphoreType.DMA((64,)),
            pltpu.SemaphoreType.DMA((3,)),
            pltpu.SemaphoreType.DMA((6,)),
        ],
        compiler_params=pltpu.CompilerParams(
            collective_id=0, has_side_effects=True, vmem_limit_bytes=48 * 1024 * 1024
        ),
        cost_estimate=pl.CostEstimate(flops=4 * 2 * ROWS * ROWS * COLS, bytes_accessed=11_000_000, transcendentals=0),
        name="exchange",
    )(momentum, gradient, right_t)


def update_kernel(ortho, scale, right, weights, momentum, gradient, new_weights, new_momentum, new_right):
    start = pl.multiple_of(lax.axis_index("tp") * 64, 64)
    basis = ortho[...]
    value = right[...]
    rh, rl = split(value)
    sh, sl = split(basis * scale[0:1, :])
    update = dot(basis.astype(BF16), rh)
    normal = dot(sh, rh) + (dot(sh, rl) + dot(sl, rh))
    new_momentum[...] = (momentum[...] + gradient[...]) - (1.0 - momentum_decay) * update
    new_weights[...] = weights[...] - learning_rate * normal
    column = jnp.broadcast_to(scale[0:1, :], (128, ROWS)).T
    both = jnp.concatenate([column] * (value.shape[1] // 128), axis=1) * value
    new_right[...] = both[0:64]
    for p in range(1, 4):
        @pl.when(start == 64 * p)
        def _(p=p):
            new_right[...] = both[64 * p : 64 * (p + 1)]


def update(ortho, scale, right, weights, momentum, gradient):
    width = 256
    whole = lambda *shape: pl.BlockSpec(shape, lambda i: (0, 0))
    block = pl.BlockSpec((ROWS, width), lambda i: (0, i))
    return pl.pallas_call(
        update_kernel,
        grid=(COLS // width,),
        out_shape=(
            jax.ShapeDtypeStruct((ROWS, COLS), F32),
            jax.ShapeDtypeStruct((ROWS, COLS), F32),
            jax.ShapeDtypeStruct((64, COLS), F32),
        ),
        in_specs=[whole(ROWS, ROWS), whole(8, ROWS), block, block, block, block],
        out_specs=(block, block, pl.BlockSpec((64, width), lambda i: (0, i))),
        compiler_params=pltpu.CompilerParams(vmem_limit_bytes=32 * 1024 * 1024),
        name="update",
    )(ortho, scale, right, weights, momentum, gradient)


def local(weights, momentum, gradient, right_factor):
    right, ortho, scale = exchange(momentum, gradient, right_factor.T)
    new_weights, new_momentum, new_right_t = update(ortho, scale, right, weights, momentum, gradient)
    return (new_weights, new_momentum, new_right_t.T)


def solution(mesh):
    return jax.shard_map(
        local,
        mesh=mesh,
        in_specs=(
            P("tp", "fsdp"),
            P(("rep", "tp"), "fsdp"),
            P(("rep", "tp"), "fsdp"),
            P("fsdp", "tp"),
        ),
        out_specs=(P("tp", "fsdp"), P(("rep", "tp"), "fsdp"), P("fsdp", "tp")),
        check_vma=False,
    )
```

time: 525 us -> 120 us (0.23)
  waiting for transfers between devices: 373 us -> 0 us
  Pallas kernels: 0 us -> 116 us
  other arithmetic: 68.9 us -> 0 us
  matrix products: 29.3 us -> 0 us
  blocking collectives: 24.4 us -> 0 us
  between operations: 15.2 us -> 0.67 us
  local copies, waits for them, and re-layouts: 12.5 us -> 3.12 us
    psum x3 -> x0, waiting for transfers between devices: 326 us -> none  [the longest x1 176 us: local(): left = lax.psum(partial_left, ('rep', 'fsdp'))]
    pallas_call x0 -> x2, Pallas kernels: none -> 116 us  [the longest x1 108 us: exchange(): pl.pallas_call(exchange_kernel, out_shape=(jax.ShapeDtypeStruct((ROWS, CO...]
    another operation x9 -> x0, other arithmetic: 58.1 us -> none  [the longest x6 35.3 us: local(): lower = jnp.linalg.cholesky(gram)]
    all_gather x1 -> x0, waiting for transfers between devices: 46.7 us -> none  [local(): lax.all_gather(right_factor, 'tp', axis=1, tiled=True)]
    psum x1 -> x0, blocking collectives: 24.4 us -> none  [local(): squares = lax.psum(jnp.sum(right_t * right_t, axis=1), 'fsdp')]
    dot_general x5 -> x0, matrix products: 22.8 us -> none  [matmul(): jnp.dot(left_side, right_side, preferred_element_type=jnp.float32, precis...]
    another operation x9 -> x0, local copies, waits for them, and re-layouts: 7.85 us -> none
    another operation x5 -> x0, matrix products: 6.52 us -> none  [the longest x3 3.71 us: local(): lax.linalg.triangular_solve(lower, left, left_side=False, lower=True, tra...]
  transfers between devices with their start and end apart: 4 -> 0, of which waited for: 4 -> 0; matrix products, arithmetic and copies ran while one was open for 1% -> 0% of each run, Pallas kernels for 0% -> 0%
where the time goes in v1:
time: 120 us
  Pallas kernels  116 us (97%)
  local copies, waits for them, and re-layouts  3.12 us (3%)
    pallas_call x1, Pallas kernels, exchange(): pl.pallas_call(exchange_kernel, out_shape=(jax.ShapeDtypeStruct((ROWS, CO...  108 us
    pallas_call x1, Pallas kernels, update(): pl.pallas_call(update_kernel, grid=(COLS // width,), out_shape=(jax.Shape...  8.42 us
    unnamed x8, local copies, waits for them, and re-layouts  3.12 us

profile of v1, /device:TPU:1, one launch (start us, length us, event | category | flops | bytes accessed | tf_op | source)
XLA Modules:
  0.0 119.8 jit_solution(4470484237511276852)
XLA Ops:
  0.6 0.0 copy-start.3
  0.6 1.1 copy-done.3
  1.8 0.0 copy-start
  1.8 0.0 copy-start.1
  1.8 107.6 %exchange.1 = (f32[256,3328]{1,0:T(8,128)S(1)}, f32[256,256]{1,0:T(8,128)S(1)}, f32[8,256]{1,0:T(8,128)S(1)}) custom-call(f32[256,3328]{1,0:T(8,128)} %momentum.3, f32[256,3328]{1,0:T(8,128)} %gradient.3, f32[64,3328]{1,0:T(8,128)S(1)} %bitcast.2), custom_call_target="tpu_custom_call" | custom-call | flops 1744830464 | bytes 11000000 | tf_op jit(solution)/shard_map/exchange/pallas_call | solution.py:367
  109.4 0.0 copy-done
  109.4 0.0 copy-done.1
  109.4 0.0 copy-start.2
  109.4 2.0 %copy-done.2 = f32[256,3328]{1,0:T(8,128)S(1)} copy-done((f32[256,3328]{1,0:T(8,128)S(1)}, f32[256,3328]{1,0:T(8,128)}, u32[]{:S(2)}) %copy-start.2) | copy-done | bytes 3407896
  111.4 8.4 %update.1 = (f32[256,3328]{1,0:T(8,128)}, f32[256,3328]{1,0:T(8,128)}, f32[64,3328]{1,0:T(8,128)}) custom-call(f32[256,256]{1,0:T(8,128)S(1)} %get-tuple-element.9.ortho, f32[8,256]{1,0:T(8,128)S(1)} %get-tuple-element.10.scale, f32[256,3328]{1,0:T(8,128)S(1)} %get-tuple-element.11.right, f32[256,3328]{1,0:T(8,128)S(1)} %copy-done.2, ...), custom_call_target="tpu_custom_call" | custom-call | tf_op jit(solution)/shard_map/update/pallas_call | solution.py:438
Async XLA Ops:
  0.6 1.2 copy-start.3
  1.8 107.6 %copy-start = (f32[256,3328]{1,0:T(8,128)S(1)}, f32[256,3328]{1,0:T(8,128)}, u32[]{:S(2)}) copy-start(f32[256,3328]{1,0:T(8,128)} %momentum.3) | copy-start | bytes 10223620
  1.8 107.6 %copy-start.1 = (f32[256,3328]{1,0:T(8,128)S(1)}, f32[256,3328]{1,0:T(8,128)}, u32[]{:S(2)}) copy-start(f32[256,3328]{1,0:T(8,128)} %gradient.3) | copy-start | bytes 10223620
  109.4 2.0 %copy-start.2 = (f32[256,3328]{1,0:T(8,128)S(1)}, f32[256,3328]{1,0:T(8,128)}, u32[]{:S(2)}) copy-start(f32[256,3328]{1,0:T(8,128)} %weights.1) | copy-start | bytes 10223620

commit v2 on v1

v2 whole, which is shorter than its diff:
```python
import functools

import jax
import jax.numpy as jnp
from jax import lax
from jax.experimental import pallas as pl
from jax.experimental.pallas import tpu as pltpu
from jax.sharding import PartitionSpec as P

MESH = pl.DeviceIdType.MESH
HIGHEST = lax.Precision.HIGHEST
F32 = jnp.float32
BF16 = jnp.bfloat16

momentum_decay = 0.95
learning_rate = 0.05
norm_eps = 1e-06

ROWS = 256
COLS = 3328
CHUNK = 832
EARLY = 512
LATE = CHUNK - EARLY
EARLY_COLS = 4 * EARLY
LATE_COLS = 4 * LATE
TOTAL_COLS = 53248
NB = 64
STEP = 8


def dot(a, b, dims=((1,), (0,)), precision=None):
    return lax.dot_general(a, b, (dims, ((), ())), precision=precision, preferred_element_type=F32)


def split(a):
    high = a.astype(BF16)
    return high, (a - high.astype(F32)).astype(BF16)


def dot3(a, b, dims=((1,), (0,))):
    ah, al = split(a)
    bh, bl = split(b)
    return dot(ah, bh, dims) + (dot(ah, bl, dims) + dot(al, bh, dims))


def cholesky_pieces(m_ref, x_ref, pivots_ref):
    n = ROWS
    rows = lax.broadcasted_iota(jnp.int32, (NB, 128), 0)
    cols = lax.broadcasted_iota(jnp.int32, (NB, 128), 1)
    eye = jnp.where(cols == rows + 64, 1.0, 0.0).astype(F32)

    def pivots_from(j):
        if j == 0:
            x_ref[...] = jnp.concatenate([m_ref[0:NB, 0:NB], jnp.zeros((NB, 128 - NB), F32)], axis=1) + eye
        x = x_ref[...]
        pivots = pivots_ref[...]
        c = [jnp.broadcast_to(x[:, j + b : j + b + 1], (NB, 128)) for b in range(STEP)]
        r = [x[j + a : j + a + 1, :] for a in range(STEP)]
        update = None
        for b in range(STEP):
            pivot = c[b][j + b : j + b + 1, :]
            pivots = jnp.where(rows == j + b, pivot, pivots)
            factor = jnp.where(rows > j + b, c[b] * (1.0 / pivot), 0.0)
            for later in range(b + 1, STEP):
                c[later] = c[later] - factor * c[later][j + b : j + b + 1, :]
                r[later] = r[later] - factor[j + later : j + later + 1, :] * r[b]
            term = factor * r[b]
            update = term if update is None else update + term
        x_ref[...] = x - update
        pivots_ref[...] = pivots

    def rest(block):
        w = (x_ref[...] * lax.rsqrt(pivots_ref[...]))[:, 64 : 64 + NB]
        m = m_ref[...]
        col = lax.broadcasted_iota(jnp.int32, (n, n), 1)
        top = dot(w, m[0:NB, :], precision=HIGHEST)
        top = jnp.concatenate([w, top[:, NB:]], axis=1)
        below = dot(m[:, 0:NB], w, ((1,), (1,)), HIGHEST)
        row = lax.broadcasted_iota(jnp.int32, (n, NB), 0)
        below = jnp.where((row >= NB) & (row < n - NB * block), below, 0.0)
        new = jnp.where(col < NB, 0.0, m) - dot(below, top, precision=HIGHEST)
        new = jnp.concatenate([new[NB:], top], axis=0)
        m_ref[...] = jnp.concatenate([new[:, NB:], new[:, :NB]], axis=1)

    pieces = []
    for block in range(n // NB):
        pieces += [functools.partial(pivots_from, j) for j in range(0, NB, STEP)]
        pieces.append(functools.partial(rest, block))
    return pieces


class Links:
    def __init__(self, send, recv):
        self.send, self.recv, self.used, self.copies = send, recv, 0, []

    def start(self, src, dst, device):
        copy = pltpu.make_async_remote_copy(
            src_ref=src,
            dst_ref=dst,
            send_sem=self.send.at[self.used],
            recv_sem=self.recv.at[self.used],
            device_id=device,
            device_id_type=MESH,
        )
        copy.start()
        self.used += 1
        self.copies.append(copy)
        return copy

    def drain(self):
        for copy in self.copies:
            copy.wait_send()


class RingSum:
    def __init__(self, links, me, to, part, relay, landing):
        self.links, self.me, self.to, self.part = links, me, to, part
        self.relay, self.landing = relay, landing
        self.right, self.left, self.far = (lax.rem(me + d, 4) for d in (1, 3, 2))

    def start(self):
        go = self.links.start
        right, left = self.to(self.right), self.to(self.left)
        self.a = go(self.part(self.far, 0), self.relay.at[0], right)
        self.b = go(self.part(self.far, 1), self.relay.at[1], left)
        self.c = go(self.part(self.right, 1), self.landing.at[0, 1], right)
        self.d = go(self.part(self.left, 0), self.landing.at[1, 0], left)

    def middle(self):
        go = self.links.start
        self.a.wait_recv()
        self.relay[0] = self.relay[0] + self.part(self.right, 0)[...]
        self.e = go(self.relay.at[0], self.landing.at[0, 0], self.to(self.right))
        self.b.wait_recv()
        self.relay[1] = self.relay[1] + self.part(self.left, 1)[...]
        self.f = go(self.relay.at[1], self.landing.at[1, 1], self.to(self.left))

    def finish(self, half):
        for copy in (self.d, self.e) if half == 0 else (self.c, self.f):
            copy.wait_recv()
        return self.part(self.me, half)[...] + (self.landing[0, half] + self.landing[1, half])


class RingGather:
    def __init__(self, links, me, to, part):
        self.links, self.me, self.to, self.part = links, me, to, part
        self.right, self.left = lax.rem(me + 1, 4), lax.rem(me + 3, 4)

    def go(self, place, half, device):
        ref = self.part(place, half)
        return self.links.start(ref, ref, self.to(device))

    def start(self):
        self.a = self.go(self.me, 0, self.right)
        self.b = self.go(self.me, 1, self.left)
        self.c = self.go(self.me, 1, self.right)
        self.d = self.go(self.me, 0, self.left)

    def middle(self):
        self.a.wait_recv()
        self.e = self.go(self.left, 0, self.right)
        self.b.wait_recv()
        self.f = self.go(self.right, 1, self.left)

    def near(self):
        self.c.wait_recv()
        self.d.wait_recv()

    def finish(self):
        self.near()
        self.e.wait_recv()
        self.f.wait_recv()


def exchange_kernel(
    momentum, gradient, right_in, right_out, ortho_out, scale_out, momentum_out,
    early, early_g, late_c, late_g, late, rown, rearly, rlate, summed, relay_b, landing_b, relay_a, landing_a,
    part_left, core_in, tiles, tiles_in, tile_out, left_tiles, left_t,
    gram_y, gram_all, chol, chol_x, chol_pivots, part_a, relay_ta, landing_ta, all_a,
    part_b, relay_tb, landing_tb, all_b, squares,
    send, recv, load, many,
):
    x, f, y = lax.axis_index("rep"), lax.axis_index("fsdp"), lax.axis_index("tp")
    z, core = f // 2, lax.rem(f, 2)
    q = x * 8 + z

    def at(x=x, z=z, core=core, y=y):
        return {"rep": x, "fsdp": z * 2 + core, "tp": y}

    def middle_out(i):
        return ((i + 1) // 2) * (1 - 2 * lax.rem(i, 2))

    def plane(i):
        there_x = lax.rem(x + 2 + middle_out(lax.rem(i, 4)), 4)
        there_z = lax.rem(z + 4 + middle_out(i // 4), 8)
        return there_x * 8 + there_z, at(x=there_x, z=there_z)

    to_x = lambda p: at(x=p)
    to_y = lambda p: at(y=p)
    partner = at(core=1 - core)
    links = Links(send, recv)

    load_r = pltpu.make_async_copy(right_in, rown, load.at[0])
    load_r.start()
    loads = []
    for p in range(4):
        cols = slice(EARLY * p, EARLY * (p + 1))
        loads.append(
            (
                pltpu.make_async_copy(momentum.at[:, cols], early.at[p], load.at[1 + 2 * p]),
                pltpu.make_async_copy(gradient.at[:, cols], early_g.at[p], load.at[2 + 2 * p]),
            )
        )
    loads.append(
        (
            pltpu.make_async_copy(momentum.at[:, EARLY_COLS:COLS], late_c, load.at[9]),
            pltpu.make_async_copy(gradient.at[:, EARLY_COLS:COLS], late_g, load.at[10]),
        )
    )
    for pair in loads:
        for copy in pair:
            copy.start()

    barrier = pltpu.get_barrier_semaphore()

    def greet(d, carry):
        pl.semaphore_signal(barrier, inc=1, device_id=plane(d)[1], device_id_type=MESH)
        return carry

    for d in (1, 2, 3):
        pl.semaphore_signal(barrier, inc=1, device_id=to_y(lax.rem(y + d, 4)), device_id_type=MESH)
    pl.semaphore_signal(barrier, inc=1, device_id=partner, device_id_type=MESH)
    lax.fori_loop(0, 31, greet, 0)

    my_ranks = pl.ds(pl.multiple_of(64 * y, 64), 64)
    load_r.wait()
    rearly[my_ranks, :] = rown[:, pl.ds(pl.multiple_of(EARLY * x, EARLY), EARLY)]
    rlate[my_ranks, :] = rown[:, EARLY_COLS:COLS]
    for p in range(4):
        for copy in loads[p]:
            copy.wait()
        early[p] = early[p] + early_g[p]
    pl.semaphore_wait(barrier, 35)

    def rank_rows(p, h):
        return pl.ds(pl.multiple_of(64 * p + 32 * h, 32), 32)

    def half(h):
        return slice(128 * h, 128 * (h + 1))

    sum_b = RingSum(links, x, to_x, lambda p, h: early.at[p, half(h)], relay_b, landing_b)
    gather_a = RingGather(links, y, to_y, lambda p, h: rlate.at[rank_rows(p, h)])
    gather_b = RingGather(links, y, to_y, lambda p, h: rearly.at[rank_rows(p, h)])
    sum_b.start()
    gather_a.start()
    gather_b.start()
    for copy in loads[4]:
        copy.wait()
    late_c[...] = late_c[...] + late_g[...]
    for p in range(4):
        late[p] = late_c[:, LATE * p : LATE * (p + 1)]
    gather_a.middle()
    sum_b.middle()
    gather_b.middle()
    gather_a.finish()
    total = dot3(late_c[...], rlate[...], ((1,), (1,)))
    gather_b.finish()
    for h in range(2):
        summed[half(h), 0:EARLY] = sum_b.finish(h)
    total = total + dot3(summed[:, 0:EARLY], rearly[...], ((1,), (1,)))
    part_left[0] = total[0:128]
    part_left[1] = total[128:256]

    swap = links.start(part_left.at[1 - core], core_in, partner)
    sum_a = RingSum(links, x, to_x, lambda p, h: late.at[p, half(h)], relay_a, landing_a)
    sum_a.start()
    swap.wait_recv()
    mine = part_left[core] + core_in[...]
    tiles[0:16] = mine[:, 0:128].reshape(16, 8, 128)
    tiles[16:32] = mine[:, 128:256].reshape(16, 8, 128)

    def scatter(d, carry):
        other, device = plane(d)
        pltpu.make_async_remote_copy(
            src_ref=tiles.at[other], dst_ref=tiles_in.at[d], send_sem=many.at[0],
            recv_sem=many.at[1], device_id=device, device_id_type=MESH,
        ).start()
        return carry

    def gather(d, carry):
        pltpu.make_async_remote_copy(
            src_ref=tile_out, dst_ref=left_tiles.at[core, q], send_sem=many.at[2],
            recv_sem=many.at[3], device_id=plane(d)[1], device_id_type=MESH,
        ).start()
        return carry

    def wait_many(i, ref):
        pltpu.make_async_copy(ref, ref, many.at[i]).wait()

    lax.fori_loop(0, 31, scatter, 0)
    wait_many(1, tiles_in)
    tile = (tiles[q] + jnp.sum(tiles_in[...], axis=0)) * 0.25
    tile_out[...] = tile
    left_tiles[core, q] = tile
    lax.fori_loop(0, 31, gather, 0)
    sum_a.middle()
    wait_many(3, tiles_in)
    swap = links.start(left_tiles.at[core], left_tiles.at[core], partner)
    for h in range(2):
        summed[half(h), EARLY:CHUNK] = sum_a.finish(h)
    swap.wait_recv()
    left = jnp.concatenate(
        [
            jnp.concatenate([left_tiles[h, 0:16].reshape(128, 128), left_tiles[h, 16:32].reshape(128, 128)], axis=1)
            for h in range(2)
        ],
        axis=0,
    )
    left_t[...] = left.T

    def y_rows(p, lo=0, n=32):
        return pl.ds(pl.multiple_of(32 * p + lo, n), n)

    class Product:
        def __init__(self, cols, part, relay, landing, whole):
            self.cols, self.part, self.whole = cols, part, whole
            self.sum = RingSum(links, y, to_y, lambda p, h: part.at[h, y_rows(p)], relay, landing)

        def multiply(self):
            for h in range(2):
                self.part[h] = dot3(left_t[half(h), :], summed[:, self.cols])

        def share(self):
            whole = self.whole
            self.first = (
                RingGather(links, y, to_y, lambda p, h: whole.at[0, x, y_rows(p, 16 * h, 16)]),
                RingGather(links, x, to_x, lambda p, h: whole.at[1, p, y_rows(y, 16 * h, 16)]),
            )
            for h in range(2):
                whole[h, x, y_rows(y), :] = self.sum.finish(h)
                self.first[h].start()

        def share_on(self):
            whole = self.whole
            for ring in self.first:
                ring.finish()
            self.then = (
                RingGather(links, x, to_x, lambda p, h: whole.at[0, p, slice(64 * h, 64 * (h + 1))]),
                RingGather(links, y, to_y, lambda p, h: whole.at[1, :, y_rows(p, 16 * h, 16)]),
            )

        def each(self, rings, step):
            for ring in rings:
                getattr(ring, step)()

    a = Product(slice(0, EARLY), part_a, relay_ta, landing_ta, all_a)
    b = Product(slice(EARLY, CHUNK), part_b, relay_tb, landing_tb, all_b)
    a.multiply()
    a.sum.start()
    b.multiply()
    slab = left_t[pl.ds(pl.multiple_of((core * 4 + x) * 32, 32), 32), :]
    gram_y[y] = dot(slab, left, precision=HIGHEST)
    grams = [links.start(gram_y.at[y], gram_y.at[y], to_y(lax.rem(y + d, 4))) for d in (2, 1, 3)]
    a.sum.middle()
    b.sum.start()
    for copy in grams:
        copy.wait_recv()
    gram_all[core, x] = (gram_y[0] + gram_y[1]) + (gram_y[2] + gram_y[3])
    grams = [links.start(gram_all.at[core, x], gram_all.at[core, x], to_x(lax.rem(x + d, 4))) for d in (2, 1, 3)]
    b.sum.middle()
    a.share()
    for copy in grams:
        copy.wait_recv()
    swap = links.start(gram_all.at[core], gram_all.at[core], partner)
    a.each(a.first, "middle")
    b.share()
    swap.wait_recv()
    for c in range(2):
        for p in range(4):
            chol[128 * c + 32 * p : 128 * c + 32 * p + 32, :] = gram_all[c, p]
    pieces = cholesky_pieces(chol, chol_x, chol_pivots)
    once = jnp.minimum(x + 1, 1)

    def work(n):
        now = [pieces.pop(0) for _ in range(n)]

        def step(i, carry):
            for piece in now:
                piece()
            return carry

        lax.fori_loop(0, once, step, 0)

    a.share_on()
    a.each(a.then, "start")
    work(3)
    b.each(b.first, "middle")
    work(8)
    b.share_on()
    a.each(a.then, "middle")
    b.each(b.then, "start")
    work(17)
    b.each(b.then, "middle")
    work(len(pieces))
    inverse = chol[...]
    ortho = dot(left, inverse, ((1,), (1,)), HIGHEST)
    ortho_out[...] = ortho

    ih, il = split(inverse * 0.25)
    sums = jnp.zeros((ROWS, 1), F32)
    for product, first, width in ((a, 0, EARLY), (b, EARLY_COLS, LATE)):
        product.each(product.then, "finish")
        for p in range(4):
            th, tl = split(jnp.concatenate([product.whole[0, p], product.whole[1, p]], axis=0))
            right = dot(ih, th) + (dot(ih, tl) + dot(il, th))
            right_out[:, first + width * p : first + width * (p + 1)] = right
            sums = sums + jnp.sum(right * right, axis=1, keepdims=True)
    squares[f] = jnp.broadcast_to(sums, (ROWS, 128)).T[0:8]

    def share(i, carry):
        there = at(z=lax.rem(z + 4 + middle_out(i // 2), 8), core=lax.rem(core + 1 + i, 2))
        pltpu.make_async_remote_copy(
            src_ref=squares.at[f], dst_ref=squares.at[f], send_sem=many.at[4],
            recv_sem=many.at[5], device_id=there, device_id_type=MESH,
        ).start()
        return carry

    lax.fori_loop(0, 15, share, 0)
    basis = ortho.astype(BF16)
    rate = 1.0 - momentum_decay
    for p in range(4):
        cols = slice(EARLY * p, EARLY * (p + 1))
        momentum_out[:, cols] = early[p] - rate * dot(basis, right_out[:, cols].astype(BF16))
    cols = slice(EARLY_COLS, COLS)
    momentum_out[:, cols] = late_c[...] - rate * dot(basis, right_out[:, cols].astype(BF16))
    wait_many(5, squares.at[0:15])
    scale_out[...] = lax.rsqrt(jnp.sum(squares[...], axis=0) / TOTAL_COLS + norm_eps)
    wait_many(0, tiles_in)
    wait_many(2, tiles_in)
    wait_many(4, squares.at[0:15])
    links.drain()


def exchange(momentum, gradient, right_t):
    vmem = lambda *shape: pltpu.VMEM(shape, F32)
    return pl.pallas_call(
        exchange_kernel,
        out_shape=(
            jax.ShapeDtypeStruct((ROWS, COLS), F32),
            jax.ShapeDtypeStruct((ROWS, ROWS), F32),
            jax.ShapeDtypeStruct((8, ROWS), F32),
            jax.ShapeDtypeStruct((ROWS, COLS), F32),
        ),
        in_specs=[pl.BlockSpec(memory_space=pltpu.HBM)] * 3,
        out_specs=(pl.BlockSpec(memory_space=pltpu.VMEM),) * 4,
        scratch_shapes=[
            vmem(4, ROWS, EARLY),
            vmem(4, ROWS, EARLY),
            vmem(ROWS, LATE_COLS),
            vmem(ROWS, LATE_COLS),
            vmem(4, ROWS, LATE),
            vmem(64, COLS),
            vmem(ROWS, EARLY),
            vmem(ROWS, LATE_COLS),
            vmem(ROWS, CHUNK),
            vmem(2, 128, EARLY),
            vmem(2, 2, 128, EARLY),
            vmem(2, 128, LATE),
            vmem(2, 2, 128, LATE),
            vmem(2, 128, ROWS),
            vmem(128, ROWS),
            vmem(32, 8, 128),
            vmem(31, 8, 128),
            vmem(8, 128),
            vmem(2, 32, 8, 128),
            vmem(ROWS, ROWS),
            vmem(4, 32, ROWS),
            vmem(2, 4, 32, ROWS),
            vmem(ROWS, ROWS),
            vmem(NB, 128),
            vmem(NB, 128),
            vmem(2, 128, EARLY),
            vmem(2, 32, EARLY),
            vmem(2, 2, 32, EARLY),
            vmem(2, 4, 128, EARLY),
            vmem(2, 128, LATE),
            vmem(2, 32, LATE),
            vmem(2, 2, 32, LATE),
            vmem(2, 4, 128, LATE),
            vmem(16, 8, ROWS),
            pltpu.SemaphoreType.DMA((128,)),
            pltpu.SemaphoreType.DMA((128,)),
            pltpu.SemaphoreType.DMA((11,)),
            pltpu.SemaphoreType.DMA((6,)),
        ],
        compiler_params=pltpu.CompilerParams(
            collective_id=0, has_side_effects=True, vmem_limit_bytes=45 * 1024 * 1024
        ),
        cost_estimate=pl.CostEstimate(flops=4 * 2 * ROWS * ROWS * COLS, bytes_accessed=11_000_000, transcendentals=0),
        name="exchange",
    )(momentum, gradient, right_t)


def update_kernel(
    ortho, scale, right, weights, momentum, new_weights, new_momentum, new_right, staged_w, column_ref, staged_r, sems
):
    copies = [pltpu.make_async_copy(momentum, new_momentum, sems.at[0])]
    copies[0].start()
    own = pl.ds(pl.multiple_of(lax.axis_index("tp") * 64, 64), 64)
    sh, sl = split(ortho[...] * scale[0:1, :])
    column_ref[...] = jnp.broadcast_to(scale[0:1, :], (128, ROWS)).T
    column = column_ref[own, :]
    column = jnp.concatenate([column] * (WIDTH // 128), axis=1)
    for i in range(COLS // WIDTH):
        cols = slice(WIDTH * i, WIDTH * (i + 1))
        rh, rl = split(right[:, cols])
        normal = dot(sh, rh) + (dot(sh, rl) + dot(sl, rh))
        staged_w[:, cols] = weights[:, cols] - learning_rate * normal
        staged_r[:, cols] = column * right[own, cols]
        copies.append(pltpu.make_async_copy(staged_w.at[:, cols], new_weights.at[:, cols], sems.at[2 * i + 1]))
        copies[-1].start()
        copies.append(
            pltpu.make_async_copy(staged_r.at[:, cols], new_right.at[:, cols], sems.at[2 * i + 2])
        )
        copies[-1].start()
    for copy in copies:
        copy.wait()


WIDTH = 1664


def update(ortho, scale, right, weights, momentum):
    return pl.pallas_call(
        update_kernel,
        out_shape=(
            jax.ShapeDtypeStruct((ROWS, COLS), F32),
            jax.ShapeDtypeStruct((ROWS, COLS), F32),
            jax.ShapeDtypeStruct((64, COLS), F32),
        ),
        in_specs=[pl.BlockSpec(memory_space=pltpu.VMEM)] * 5,
        out_specs=(pl.BlockSpec(memory_space=pltpu.HBM),) * 3,
        scratch_shapes=[
            pltpu.VMEM((ROWS, COLS), F32),
            pltpu.VMEM((ROWS, 128), F32),
            pltpu.VMEM((64, COLS), F32),
            pltpu.SemaphoreType.DMA((2 * (COLS // WIDTH) + 1,)),
        ],
        compiler_params=pltpu.CompilerParams(vmem_limit_bytes=40 * 1024 * 1024),
        name="update",
    )(ortho, scale, right, weights, momentum)


def local(weights, momentum, gradient, right_factor):
    right, ortho, scale, moved = exchange(momentum, gradient, right_factor.T)
    new_weights, new_momentum, new_right_t = update(ortho, scale, right, weights, moved)
    return (new_weights, new_momentum, new_right_t.T)


def solution(mesh):
    return jax.shard_map(
        local,
        mesh=mesh,
        in_specs=(
            P("tp", "fsdp"),
            P(("rep", "tp"), "fsdp"),
            P(("rep", "tp"), "fsdp"),
            P("fsdp", "tp"),
        ),
        out_specs=(P("tp", "fsdp"), P(("rep", "tp"), "fsdp"), P("fsdp", "tp")),
        check_vma=False,
    )
```

time: 120 us -> 102 us (0.85)
  Pallas kernels: 116 us -> 99.6 us
  local copies, waits for them, and re-layouts: 3.12 us -> 1.15 us
    pallas_call x1, Pallas kernels: 108 us -> 96.5 us  [exchange(): pl.pallas_call(exchange_kernel, out_shape=(jax.ShapeDtypeStruct((ROWS, CO...]
    pallas_call x1, Pallas kernels: 8.42 us -> 3.13 us  [update(): pl.pallas_call(update_kernel, out_shape=(jax.ShapeDtypeStruct((ROWS, COLS...]
    unnamed x8 -> x4, local copies, waits for them, and re-layouts: 3.12 us -> 1.15 us
where the time goes in v2:
time: 102 us
  Pallas kernels  99.6 us (98%)
  local copies, waits for them, and re-layouts  1.15 us (1%)
    pallas_call x1, Pallas kernels, exchange(): pl.pallas_call(exchange_kernel, out_shape=(jax.ShapeDtypeStruct((ROWS, CO...  96.5 us
    pallas_call x1, Pallas kernels, update(): pl.pallas_call(update_kernel, out_shape=(jax.ShapeDtypeStruct((ROWS, COLS...  3.13 us

profile of v2, /device:TPU:1, one launch (start us, length us, event | category | flops | bytes accessed | tf_op | source)
XLA Modules:
  0.0 101.6 jit_solution(8061516100376703994)
XLA Ops:
  0.6 0.0 copy-start.1
  0.6 1.1 %copy-done.1 = f32[3328,64]{0,1:T(8,128)S(1)} copy-done((f32[3328,64]{0,1:T(8,128)S(1)}, f32[3328,64]{0,1:T(8,128)}, u32[]{:S(2)}) %copy-start.1) | copy-done | bytes 851992
  1.8 0.0 copy-start
  1.8 96.5 %exchange.1 = (f32[256,3328]{1,0:T(8,128)S(1)}, f32[256,256]{1,0:T(8,128)S(1)}, f32[8,256]{1,0:T(8,128)S(1)}, f32[256,3328]{1,0:T(8,128)S(1)}) custom-call(f32[256,3328]{1,0:T(8,128)} %momentum.1, f32[256,3328]{1,0:T(8,128)} %gradient.1, f32[64,3328]{1,0:T(8,128)S(1)} %bitcast.2), custom_call_target="tpu_custom_call" | custom-call | flops 1744830464 | bytes 11000000 | tf_op jit(solution)/shard_map/exchange/pallas_call | solution.py:446
  98.3 0.0 copy-done
  98.3 3.1 %update.1 = (f32[256,3328]{1,0:T(8,128)}, f32[256,3328]{1,0:T(8,128)}, f32[64,3328]{1,0:T(8,128)}) custom-call(f32[256,256]{1,0:T(8,128)S(1)} %get-tuple-element.10.ortho, f32[8,256]{1,0:T(8,128)S(1)} %get-tuple-element.11.scale, f32[256,3328]{1,0:T(8,128)S(1)} %get-tuple-element.12.right, f32[256,3328]{1,0:T(8,128)S(1)} %copy-done, ...), custom_call_target="tpu_custom_call" | custom-call | tf_op jit(solution)/shard_map/update/pallas_call | solution.py:534
Async XLA Ops:
  0.6 1.2 %copy-start.1 = (f32[3328,64]{0,1:T(8,128)S(1)}, f32[3328,64]{0,1:T(8,128)}, u32[]{:S(2)}) copy-start(f32[3328,64]{0,1:T(8,128)} %param.7) | copy-start | bytes 2555908
  1.8 96.5 %copy-start = (f32[256,3328]{1,0:T(8,128)S(1)}, f32[256,3328]{1,0:T(8,128)}, u32[]{:S(2)}) copy-start(f32[256,3328]{1,0:T(8,128)} %weights.1) | copy-start | bytes 10223620

commit v3 on v2

--- a/solution.py
+++ b/solution.py
@@ -24,6 +24,8 @@
 EARLY_COLS = 4 * EARLY
 LATE_COLS = 4 * LATE
 TOTAL_COLS = 53248
+SHARES = (40, 24)
+SENDS, ARRIVALS = 19, 53
 NB = 64
 STEP = 8
 
@@ -91,85 +93,102 @@
 
 class Links:
     def __init__(self, send, recv):
-        self.send, self.recv, self.used, self.copies = send, recv, 0, []
-
-    def start(self, src, dst, device):
+        self.send, self.recv, self.sends, self.recvs, self.at_end = send, recv, 0, 0, []
+
+    def wait(self, sem, ref):
+        pltpu.make_async_copy(ref, ref, sem).wait()
+
+    def group(self, ref):
+        sem = self.send.at[self.sends]
+        self.sends += 1
+        self.at_end.append(lambda: self.wait(sem, ref))
+        return sem
+
+    def arrivals(self):
+        sem = self.recv.at[self.recvs]
+        self.recvs += 1
+        return sem
+
+    def start(self, src, dst, device, group=None, arrivals=None):
+        alone = group is None
+        if alone:
+            group = self.send.at[self.sends]
+            self.sends += 1
         copy = pltpu.make_async_remote_copy(
             src_ref=src,
             dst_ref=dst,
-            send_sem=self.send.at[self.used],
-            recv_sem=self.recv.at[self.used],
+            send_sem=group,
+            recv_sem=self.arrivals() if arrivals is None else arrivals,
             device_id=device,
             device_id_type=MESH,
         )
         copy.start()
-        self.used += 1
-        self.copies.append(copy)
+        if alone:
+            self.at_end.append(copy.wait_send)
         return copy
 
     def drain(self):
-        for copy in self.copies:
-            copy.wait_send()
+        for wait in self.at_end:
+            wait()
 
 
 class RingSum:
-    def __init__(self, links, me, to, part, relay, landing):
+    def __init__(self, links, me, to, part, relay, landing, sent):
         self.links, self.me, self.to, self.part = links, me, to, part
         self.relay, self.landing = relay, landing
         self.right, self.left, self.far = (lax.rem(me + d, 4) for d in (1, 3, 2))
+        self.group = links.group(sent)
+
+    def go(self, src, dst, place):
+        return self.links.start(src, dst, self.to(place), self.group)
 
     def start(self):
-        go = self.links.start
-        right, left = self.to(self.right), self.to(self.left)
-        self.a = go(self.part(self.far, 0), self.relay.at[0], right)
-        self.b = go(self.part(self.far, 1), self.relay.at[1], left)
-        self.c = go(self.part(self.right, 1), self.landing.at[0, 1], right)
-        self.d = go(self.part(self.left, 0), self.landing.at[1, 0], left)
+        self.start_far()
+        self.start_near()
+
+    def start_far(self):
+        self.a = self.go(self.part(self.far, 0), self.relay(0), self.right)
+        self.b = self.go(self.part(self.far, 1), self.relay(1), self.left)
+
+    def start_near(self):
+        self.c = self.go(self.part(self.right, 1), self.landing(0, 1), self.right)
+        self.d = self.go(self.part(self.left, 0), self.landing(1, 0), self.left)
 
     def middle(self):
-        go = self.links.start
         self.a.wait_recv()
-        self.relay[0] = self.relay[0] + self.part(self.right, 0)[...]
-        self.e = go(self.relay.at[0], self.landing.at[0, 0], self.to(self.right))
+        ref = self.relay(0)
+        ref[...] = ref[...] + self.part(self.right, 0)[...]
+        self.e = self.go(ref, self.landing(0, 0), self.right)
         self.b.wait_recv()
-        self.relay[1] = self.relay[1] + self.part(self.left, 1)[...]
-        self.f = go(self.relay.at[1], self.landing.at[1, 1], self.to(self.left))
+        ref = self.relay(1)
+        ref[...] = ref[...] + self.part(self.left, 1)[...]
+        self.f = self.go(ref, self.landing(1, 1), self.left)
 
     def finish(self, half):
         for copy in (self.d, self.e) if half == 0 else (self.c, self.f):
             copy.wait_recv()
-        return self.part(self.me, half)[...] + (self.landing[0, half] + self.landing[1, half])
+        return self.part(self.me, half)[...] + (self.landing(0, half)[...] + self.landing(1, half)[...])
 
 
 class RingGather:
-    def __init__(self, links, me, to, part):
+    def __init__(self, links, me, to, part, group, first, rest):
         self.links, self.me, self.to, self.part = links, me, to, part
+        self.group, self.first, self.rest = group, first, rest
         self.right, self.left = lax.rem(me + 1, 4), lax.rem(me + 3, 4)
 
-    def go(self, place, half, device):
+    def go(self, place, half, device, arrivals):
         ref = self.part(place, half)
-        return self.links.start(ref, ref, self.to(device))
+        self.links.start(ref, ref, self.to(device), self.group, arrivals)
 
     def start(self):
-        self.a = self.go(self.me, 0, self.right)
-        self.b = self.go(self.me, 1, self.left)
-        self.c = self.go(self.me, 1, self.right)
-        self.d = self.go(self.me, 0, self.left)
-
-    def middle(self):
-        self.a.wait_recv()
-        self.e = self.go(self.left, 0, self.right)
-        self.b.wait_recv()
-        self.f = self.go(self.right, 1, self.left)
-
-    def near(self):
-        self.c.wait_recv()
-        self.d.wait_recv()
-
-    def finish(self):
-        self.near()
-        self.e.wait_recv()
-        self.f.wait_recv()
+        self.go(self.me, 0, self.right, self.first)
+        self.go(self.me, 1, self.left, self.first)
+        self.go(self.me, 1, self.right, self.rest)
+        self.go(self.me, 0, self.left, self.rest)
+
+    def forward(self):
+        self.go(self.left, 0, self.right, self.rest)
+        self.go(self.right, 1, self.left, self.rest)
 
 
 def exchange_kernel(
@@ -202,13 +221,14 @@
 
     load_r = pltpu.make_async_copy(right_in, rown, load.at[0])
     load_r.start()
+    order = [lax.rem(x + d, 4) for d in (2, 1, 3, 0)]
     loads = []
-    for p in range(4):
-        cols = slice(EARLY * p, EARLY * (p + 1))
+    for i, p in enumerate(order):
+        cols = pl.ds(pl.multiple_of(EARLY * p, EARLY), EARLY)
         loads.append(
             (
-                pltpu.make_async_copy(momentum.at[:, cols], early.at[p], load.at[1 + 2 * p]),
-                pltpu.make_async_copy(gradient.at[:, cols], early_g.at[p], load.at[2 + 2 * p]),
+                pltpu.make_async_copy(momentum.at[:, cols], early.at[p], load.at[1 + 2 * i]),
+                pltpu.make_async_copy(gradient.at[:, cols], early_g.at[p], load.at[2 + 2 * i]),
             )
         )
     loads.append(
@@ -217,9 +237,14 @@
             pltpu.make_async_copy(gradient.at[:, EARLY_COLS:COLS], late_g, load.at[10]),
         )
     )
-    for pair in loads:
+    for pair in loads[:4]:
         for copy in pair:
             copy.start()
+
+    def loaded(i):
+        for copy in loads[i]:
+            copy.wait()
+        early[order[i]] = early[order[i]] + early_g[order[i]]
 
     barrier = pltpu.get_barrier_semaphore()
 
@@ -236,10 +261,7 @@
     load_r.wait()
     rearly[my_ranks, :] = rown[:, pl.ds(pl.multiple_of(EARLY * x, EARLY), EARLY)]
     rlate[my_ranks, :] = rown[:, EARLY_COLS:COLS]
-    for p in range(4):
-        for copy in loads[p]:
-            copy.wait()
-        early[p] = early[p] + early_g[p]
+    loaded(0)
     pl.semaphore_wait(barrier, 35)
 
     def rank_rows(p, h):
@@ -248,23 +270,37 @@
     def half(h):
         return slice(128 * h, 128 * (h + 1))
 
-    sum_b = RingSum(links, x, to_x, lambda p, h: early.at[p, half(h)], relay_b, landing_b)
-    gather_a = RingGather(links, y, to_y, lambda p, h: rlate.at[rank_rows(p, h)])
-    gather_b = RingGather(links, y, to_y, lambda p, h: rearly.at[rank_rows(p, h)])
-    sum_b.start()
+    sum_b = RingSum(
+        links, x, to_x, lambda p, h: early.at[p, half(h)],
+        lambda h: relay_b.at[h], lambda i, h: landing_b.at[i, h], early.at[0:3],
+    )
+    gathers = []
+    for ref in (rlate, rearly):
+        sems = (links.group(ref.at[0:192]), links.arrivals(), links.arrivals())
+        gathers.append(RingGather(links, y, to_y, lambda p, h, ref=ref: ref.at[rank_rows(p, h)], *sems))
+    gather_a, gather_b = gathers
+    sum_b.start_far()
     gather_a.start()
     gather_b.start()
+    loaded(1)
+    loaded(2)
+    sum_b.start_near()
+    for copy in loads[4]:
+        copy.start()
+    loaded(3)
     for copy in loads[4]:
         copy.wait()
     late_c[...] = late_c[...] + late_g[...]
     for p in range(4):
         late[p] = late_c[:, LATE * p : LATE * (p + 1)]
-    gather_a.middle()
+    links.wait(gather_a.first, rlate.at[0:64])
+    gather_a.forward()
     sum_b.middle()
-    gather_b.middle()
-    gather_a.finish()
+    links.wait(gather_b.first, rearly.at[0:64])
+    gather_b.forward()
+    links.wait(gather_a.rest, rlate.at[0:128])
     total = dot3(late_c[...], rlate[...], ((1,), (1,)))
-    gather_b.finish()
+    links.wait(gather_b.rest, rearly.at[0:128])
     for h in range(2):
         summed[half(h), 0:EARLY] = sum_b.finish(h)
     total = total + dot3(summed[:, 0:EARLY], rearly[...], ((1,), (1,)))
@@ -272,8 +308,10 @@
     part_left[1] = total[128:256]
 
     swap = links.start(part_left.at[1 - core], core_in, partner)
-    sum_a = RingSum(links, x, to_x, lambda p, h: late.at[p, half(h)], relay_a, landing_a)
-    sum_a.start()
+    sum_a = RingSum(
+        links, x, to_x, lambda p, h: late.at[p, half(h)],
+        lambda h: relay_a.at[h], lambda i, h: landing_a.at[i, h], late.at[0:3],
+    )
     swap.wait_recv()
     mine = part_left[core] + core_in[...]
     tiles[0:16] = mine[:, 0:128].reshape(16, 8, 128)
@@ -298,16 +336,16 @@
         pltpu.make_async_copy(ref, ref, many.at[i]).wait()
 
     lax.fori_loop(0, 31, scatter, 0)
+    sum_a.start_far()
     wait_many(1, tiles_in)
     tile = (tiles[q] + jnp.sum(tiles_in[...], axis=0)) * 0.25
     tile_out[...] = tile
     left_tiles[core, q] = tile
     lax.fori_loop(0, 31, gather, 0)
+    sum_a.start_near()
     sum_a.middle()
     wait_many(3, tiles_in)
     swap = links.start(left_tiles.at[core], left_tiles.at[core], partner)
-    for h in range(2):
-        summed[half(h), EARLY:CHUNK] = sum_a.finish(h)
     swap.wait_recv()
     left = jnp.concatenate(
         [
@@ -318,51 +356,78 @@
     )
     left_t[...] = left.T
 
-    def y_rows(p, lo=0, n=32):
-        return pl.ds(pl.multiple_of(32 * p + lo, n), n)
+    def ranks(p, h, part=None):
+        n = SHARES[h]
+        low, count = ((0, n), (0, n // 16 * 8 + 8), (n // 16 * 8 + 8, n - n // 16 * 8 - 8))[0 if part is None else part + 1]
+        return pl.ds(pl.multiple_of((0, 4 * SHARES[0])[h] + n * p + low, 8), count)
 
     class Product:
-        def __init__(self, cols, part, relay, landing, whole):
-            self.cols, self.part, self.whole = cols, part, whole
-            self.sum = RingSum(links, y, to_y, lambda p, h: part.at[h, y_rows(p)], relay, landing)
+        def __init__(self, cols, like, part, relay, landing, whole):
+            self.cols, self.like, self.part, self.whole = cols, like, part, whole
+            first = (0, SHARES[0])
+
+            def rows(h):
+                return slice(first[h], first[h] + SHARES[h])
+
+            self.sum = RingSum(
+                links, y, to_y, lambda p, h: part.at[ranks(p, h)],
+                lambda h: relay.at[rows(h)], lambda i, h: landing.at[i, rows(h)], like.at[0, 0:192],
+            )
+            self.group_1, self.group_2 = links.group(like.at[0, 0:192]), links.group(like.at[0:3])
+            self.from_place = {d: links.arrivals() for d in (1, 2, 3)}
+            self.first = {d: links.arrivals() for d in range(4)}
+            self.rest = links.arrivals()
+            self.rings = {}
 
         def multiply(self):
+            self.part[...] = dot3(left_t[...], summed[:, self.cols])
+
+        def share(self):
             for h in range(2):
-                self.part[h] = dot3(left_t[half(h), :], summed[:, self.cols])
-
-        def share(self):
+                piece = self.whole.at[x, ranks(y, h)]
+                piece[...] = self.sum.finish(h)
+                for d in (1, 3, 2):
+                    there = to_y(lax.rem(y + d, 4)) if h == 0 else to_x(lax.rem(x + d, 4))
+                    links.start(piece, piece, there, self.group_1, self.from_place[4 - d])
+            self.pass_on(0)
+
+        def pass_on(self, d):
             whole = self.whole
-            self.first = (
-                RingGather(links, y, to_y, lambda p, h: whole.at[0, x, y_rows(p, 16 * h, 16)]),
-                RingGather(links, x, to_x, lambda p, h: whole.at[1, p, y_rows(y, 16 * h, 16)]),
+            from_y, from_x = lax.rem(y + d, 4), lax.rem(x + d, 4)
+            sems = (self.group_2, self.first[d], self.rest)
+            self.rings[d] = (
+                RingGather(links, x, to_x, lambda p, i: whole.at[p, ranks(from_y, 0, i)], *sems),
+                RingGather(links, y, to_y, lambda p, i: whole.at[from_x, ranks(p, 1, i)], *sems),
             )
-            for h in range(2):
-                whole[h, x, y_rows(y), :] = self.sum.finish(h)
-                self.first[h].start()
-
-        def share_on(self):
-            whole = self.whole
-            for ring in self.first:
-                ring.finish()
-            self.then = (
-                RingGather(links, x, to_x, lambda p, h: whole.at[0, p, slice(64 * h, 64 * (h + 1))]),
-                RingGather(links, y, to_y, lambda p, h: whole.at[1, :, y_rows(p, 16 * h, 16)]),
-            )
-
-        def each(self, rings, step):
-            for ring in rings:
-                getattr(ring, step)()
-
-    a = Product(slice(0, EARLY), part_a, relay_ta, landing_ta, all_a)
-    b = Product(slice(EARLY, CHUNK), part_b, relay_tb, landing_tb, all_b)
+            for ring in self.rings[d]:
+                ring.start()
+
+        def arrived(self, *places):
+            for d in places:
+                links.wait(self.from_place[d], self.like.at[0, 0:64])
+                self.pass_on(d)
+
+        def forward(self, *places):
+            for d in places:
+                links.wait(self.first[d], self.like.at[0, 0:64])
+                for ring in self.rings[d]:
+                    ring.forward()
+
+        def finish(self):
+            links.wait(self.rest, self.like.at[0:2])
+
+    a = Product(slice(0, EARLY), early, part_a, relay_ta, landing_ta, all_a)
+    b = Product(slice(EARLY, CHUNK), late, part_b, relay_tb, landing_tb, all_b)
     a.multiply()
     a.sum.start()
-    b.multiply()
     slab = left_t[pl.ds(pl.multiple_of((core * 4 + x) * 32, 32), 32), :]
     gram_y[y] = dot(slab, left, precision=HIGHEST)
     grams = [links.start(gram_y.at[y], gram_y.at[y], to_y(lax.rem(y + d, 4))) for d in (2, 1, 3)]
+    for h in range(2):
+        summed[half(h), EARLY:CHUNK] = sum_a.finish(h)
+    b.multiply()
+    b.sum.start()
     a.sum.middle()
-    b.sum.start()
     for copy in grams:
         copy.wait_recv()
     gram_all[core, x] = (gram_y[0] + gram_y[1]) + (gram_y[2] + gram_y[3])
@@ -372,7 +437,6 @@
     for copy in grams:
         copy.wait_recv()
     swap = links.start(gram_all.at[core], gram_all.at[core], partner)
-    a.each(a.first, "middle")
     b.share()
     swap.wait_recv()
     for c in range(2):
@@ -391,16 +455,21 @@
 
         lax.fori_loop(0, once, step, 0)
 
-    a.share_on()
-    a.each(a.then, "start")
     work(3)
-    b.each(b.first, "middle")
-    work(8)
-    b.share_on()
-    a.each(a.then, "middle")
-    b.each(b.then, "start")
-    work(17)
-    b.each(b.then, "middle")
+    a.arrived(1, 3)
+    work(3)
+    b.arrived(1, 3)
+    a.forward(0)
+    a.arrived(2)
+    work(3)
+    b.arrived(2)
+    b.forward(0)
+    work(5)
+    a.forward(1, 3)
+    b.forward(1, 3)
+    work(6)
+    a.forward(2)
+    b.forward(2)
     work(len(pieces))
     inverse = chol[...]
     ortho = dot(left, inverse, ((1,), (1,)), HIGHEST)
@@ -409,13 +478,13 @@
     ih, il = split(inverse * 0.25)
     sums = jnp.zeros((ROWS, 1), F32)
     for product, first, width in ((a, 0, EARLY), (b, EARLY_COLS, LATE)):
-        product.each(product.then, "finish")
+        product.finish()
         for p in range(4):
-            th, tl = split(jnp.concatenate([product.whole[0, p], product.whole[1, p]], axis=0))
+            th, tl = split(product.whole[p])
             right = dot(ih, th) + (dot(ih, tl) + dot(il, th))
             right_out[:, first + width * p : first + width * (p + 1)] = right
             sums = sums + jnp.sum(right * right, axis=1, keepdims=True)
-    squares[f] = jnp.broadcast_to(sums, (ROWS, 128)).T[0:8]
+    squares[f] = jnp.broadcast_to(sums, (ROWS, 128)).T[0:1]
 
     def share(i, carry):
         there = at(z=lax.rem(z + 4 + middle_out(i // 2), 8), core=lax.rem(core + 1 + i, 2))
@@ -434,11 +503,13 @@
     cols = slice(EARLY_COLS, COLS)
     momentum_out[:, cols] = late_c[...] - rate * dot(basis, right_out[:, cols].astype(BF16))
     wait_many(5, squares.at[0:15])
-    scale_out[...] = lax.rsqrt(jnp.sum(squares[...], axis=0) / TOTAL_COLS + norm_eps)
+    total = jnp.sum(squares[...], axis=0)
+    scale_out[...] = jnp.broadcast_to(lax.rsqrt(total / TOTAL_COLS + norm_eps), (8, ROWS))
     wait_many(0, tiles_in)
     wait_many(2, tiles_in)
     wait_many(4, squares.at[0:15])
     links.drain()
+    assert links.sends <= SENDS and links.recvs <= ARRIVALS
 
 
 def exchange(momentum, gradient, right_t):
@@ -479,17 +550,17 @@
             vmem(ROWS, ROWS),
             vmem(NB, 128),
             vmem(NB, 128),
-            vmem(2, 128, EARLY),
-            vmem(2, 32, EARLY),
-            vmem(2, 2, 32, EARLY),
-            vmem(2, 4, 128, EARLY),
-            vmem(2, 128, LATE),
-            vmem(2, 32, LATE),
-            vmem(2, 2, 32, LATE),
-            vmem(2, 4, 128, LATE),
-            vmem(16, 8, ROWS),
-            pltpu.SemaphoreType.DMA((128,)),
-            pltpu.SemaphoreType.DMA((128,)),
+            vmem(ROWS, EARLY),
+            vmem(64, EARLY),
+            vmem(2, 64, EARLY),
+            vmem(4, ROWS, EARLY),
+            vmem(ROWS, LATE),
+            vmem(64, LATE),
+            vmem(2, 64, LATE),
+            vmem(4, ROWS, LATE),
+            vmem(16, 1, ROWS),
+            pltpu.SemaphoreType.DMA((SENDS,)),
+            pltpu.SemaphoreType.DMA((ARRIVALS,)),
             pltpu.SemaphoreType.DMA((11,)),
             pltpu.SemaphoreType.DMA((6,)),
         ],

time: 102 us -> 97.5 us (0.956)
  Pallas kernels: 99.6 us -> 95.4 us
    pallas_call x1, Pallas kernels: 96.5 us -> 92.3 us  [exchange(): pl.pallas_call(exchange_kernel, out_shape=(jax.ShapeDtypeStruct((ROWS, CO...]
where the time goes in v3:
time: 97.5 us; the launch traced here: 97.4 us
  Pallas kernels  95.4 us (98%)
  local copies, waits for them, and re-layouts  1.15 us (1%)
    pallas_call x1, Pallas kernels, exchange(): pl.pallas_call(exchange_kernel, out_shape=(jax.ShapeDtypeStruct((ROWS, CO...  92.3 us
    pallas_call x1, Pallas kernels, update(): pl.pallas_call(update_kernel, out_shape=(jax.ShapeDtypeStruct((ROWS, COLS...  3.13 us

profile of v3, /device:TPU:1, one launch (start us, length us, event | category | flops | bytes accessed | tf_op | source)
XLA Modules:
  0.0 97.4 jit_solution(7395891846866489305)
XLA Ops:
  0.6 0.0 copy-start.1
  0.6 1.1 %copy-done.1 = f32[3328,64]{0,1:T(8,128)S(1)} copy-done((f32[3328,64]{0,1:T(8,128)S(1)}, f32[3328,64]{0,1:T(8,128)}, u32[]{:S(2)}) %copy-start.1) | copy-done | bytes 851992
  1.8 0.0 copy-start
  1.8 92.3 %exchange.1 = (f32[256,3328]{1,0:T(8,128)S(1)}, f32[256,256]{1,0:T(8,128)S(1)}, f32[8,256]{1,0:T(8,128)S(1)}, f32[256,3328]{1,0:T(8,128)S(1)}) custom-call(f32[256,3328]{1,0:T(8,128)} %momentum.1, f32[256,3328]{1,0:T(8,128)} %gradient.1, f32[64,3328]{1,0:T(8,128)S(1)} %bitcast.2), custom_call_target="tpu_custom_call" | custom-call | flops 1744830464 | bytes 11000000 | tf_op jit(solution)/shard_map/exchange/pallas_call | solution.py:517
  94.1 0.0 copy-done
  94.1 3.1 %update.1 = (f32[256,3328]{1,0:T(8,128)}, f32[256,3328]{1,0:T(8,128)}, f32[64,3328]{1,0:T(8,128)}) custom-call(f32[256,256]{1,0:T(8,128)S(1)} %get-tuple-element.10.ortho, f32[8,256]{1,0:T(8,128)S(1)} %get-tuple-element.11.scale, f32[256,3328]{1,0:T(8,128)S(1)} %get-tuple-element.12.right, f32[256,3328]{1,0:T(8,128)S(1)} %copy-done, ...), custom_call_target="tpu_custom_call" | custom-call | tf_op jit(solution)/shard_map/update/pallas_call | solution.py:605
Async XLA Ops:
  0.6 1.2 %copy-start.1 = (f32[3328,64]{0,1:T(8,128)S(1)}, f32[3328,64]{0,1:T(8,128)}, u32[]{:S(2)}) copy-start(f32[3328,64]{0,1:T(8,128)} %param.7) | copy-start | bytes 2555908
  1.8 92.3 %copy-start = (f32[256,3328]{1,0:T(8,128)S(1)}, f32[256,3328]{1,0:T(8,128)}, u32[]{:S(2)}) copy-start(f32[256,3328]{1,0:T(8,128)} %weights.1) | copy-start | bytes 10223620

commit v4 on v3

--- a/solution.py
+++ b/solution.py
@@ -24,7 +24,7 @@
 EARLY_COLS = 4 * EARLY
 LATE_COLS = 4 * LATE
 TOTAL_COLS = 53248
-SHARES = (40, 24)
+SHARES = (32, 32)
 SENDS, ARRIVALS = 19, 53
 NB = 64
 STEP = 8

time: 97.5 us -> 96 us (0.985)
  Pallas kernels: 95.4 us -> 93.8 us
    pallas_call x1, Pallas kernels: 92.3 us -> 90.7 us  [exchange(): pl.pallas_call(exchange_kernel, out_shape=(jax.ShapeDtypeStruct((ROWS, CO...]
where the time goes in v4:
time: 96 us; the launch traced here: 95.8 us
  Pallas kernels  93.8 us (98%)
  local copies, waits for them, and re-layouts  1.15 us (1%)
    pallas_call x1, Pallas kernels, exchange(): pl.pallas_call(exchange_kernel, out_shape=(jax.ShapeDtypeStruct((ROWS, CO...  90.7 us
    pallas_call x1, Pallas kernels, update(): pl.pallas_call(update_kernel, out_shape=(jax.ShapeDtypeStruct((ROWS, COLS...  3.13 us

profile of v4, /device:TPU:1, one launch (start us, length us, event | category | flops | bytes accessed | tf_op | source)
XLA Modules:
  0.0 95.8 jit_solution(7886098249718288827)
XLA Ops:
  0.6 0.0 copy-start.1
  0.6 1.1 %copy-done.1 = f32[3328,64]{0,1:T(8,128)S(1)} copy-done((f32[3328,64]{0,1:T(8,128)S(1)}, f32[3328,64]{0,1:T(8,128)}, u32[]{:S(2)}) %copy-start.1) | copy-done | bytes 851992
  1.8 0.0 copy-start
  1.8 90.7 %exchange.1 = (f32[256,3328]{1,0:T(8,128)S(1)}, f32[256,256]{1,0:T(8,128)S(1)}, f32[8,256]{1,0:T(8,128)S(1)}, f32[256,3328]{1,0:T(8,128)S(1)}) custom-call(f32[256,3328]{1,0:T(8,128)} %momentum.1, f32[256,3328]{1,0:T(8,128)} %gradient.1, f32[64,3328]{1,0:T(8,128)S(1)} %bitcast.2), custom_call_target="tpu_custom_call" | custom-call | flops 1744830464 | bytes 11000000 | tf_op jit(solution)/shard_map/exchange/pallas_call | solution.py:517
  92.5 0.0 copy-done
  92.5 3.1 %update.1 = (f32[256,3328]{1,0:T(8,128)}, f32[256,3328]{1,0:T(8,128)}, f32[64,3328]{1,0:T(8,128)}) custom-call(f32[256,256]{1,0:T(8,128)S(1)} %get-tuple-element.10.ortho, f32[8,256]{1,0:T(8,128)S(1)} %get-tuple-element.11.scale, f32[256,3328]{1,0:T(8,128)S(1)} %get-tuple-element.12.right, f32[256,3328]{1,0:T(8,128)S(1)} %copy-done, ...), custom_call_target="tpu_custom_call" | custom-call | tf_op jit(solution)/shard_map/update/pallas_call | solution.py:605
Async XLA Ops:
  0.6 1.2 %copy-start.1 = (f32[3328,64]{0,1:T(8,128)S(1)}, f32[3328,64]{0,1:T(8,128)}, u32[]{:S(2)}) copy-start(f32[3328,64]{0,1:T(8,128)} %param.7) | copy-start | bytes 2555908
  1.8 90.7 %copy-start = (f32[256,3328]{1,0:T(8,128)S(1)}, f32[256,3328]{1,0:T(8,128)}, u32[]{:S(2)}) copy-start(f32[256,3328]{1,0:T(8,128)} %weights.1) | copy-start | bytes 10223620

commit v5 on v4

--- a/solution.py
+++ b/solution.py
@@ -193,7 +193,7 @@
 
 def exchange_kernel(
     momentum, gradient, right_in, right_out, ortho_out, scale_out, momentum_out,
-    early, early_g, late_c, late_g, late, rown, rearly, rlate, summed, relay_b, landing_b, relay_a, landing_a,
+    early, early_g, late_c, late_g, late, rearly, rlate, summed, relay_b, landing_b, relay_a, landing_a,
     part_left, core_in, tiles, tiles_in, tile_out, left_tiles, left_t,
     gram_y, gram_all, chol, chol_x, chol_pivots, part_a, relay_ta, landing_ta, all_a,
     part_b, relay_tb, landing_tb, all_b, squares,
@@ -219,22 +219,31 @@
     partner = at(core=1 - core)
     links = Links(send, recv)
 
-    load_r = pltpu.make_async_copy(right_in, rown, load.at[0])
-    load_r.start()
+    barrier = pltpu.get_barrier_semaphore()
+
+    def greet(d, carry):
+        pl.semaphore_signal(barrier, inc=1, device_id=plane(d)[1], device_id_type=MESH)
+        return carry
+
+    for d in (1, 2, 3):
+        pl.semaphore_signal(barrier, inc=1, device_id=to_y(lax.rem(y + d, 4)), device_id_type=MESH)
+    pl.semaphore_signal(barrier, inc=1, device_id=partner, device_id_type=MESH)
+    lax.fori_loop(0, 31, greet, 0)
+
     order = [lax.rem(x + d, 4) for d in (2, 1, 3, 0)]
     loads = []
     for i, p in enumerate(order):
         cols = pl.ds(pl.multiple_of(EARLY * p, EARLY), EARLY)
         loads.append(
             (
-                pltpu.make_async_copy(momentum.at[:, cols], early.at[p], load.at[1 + 2 * i]),
-                pltpu.make_async_copy(gradient.at[:, cols], early_g.at[p], load.at[2 + 2 * i]),
+                pltpu.make_async_copy(momentum.at[:, cols], early.at[p], load.at[2 * i]),
+                pltpu.make_async_copy(gradient.at[:, cols], early_g.at[p], load.at[2 * i + 1]),
             )
         )
     loads.append(
         (
-            pltpu.make_async_copy(momentum.at[:, EARLY_COLS:COLS], late_c, load.at[9]),
-            pltpu.make_async_copy(gradient.at[:, EARLY_COLS:COLS], late_g, load.at[10]),
+            pltpu.make_async_copy(momentum.at[:, EARLY_COLS:COLS], late_c, load.at[8]),
+            pltpu.make_async_copy(gradient.at[:, EARLY_COLS:COLS], late_g, load.at[9]),
         )
     )
     for pair in loads[:4]:
@@ -246,21 +255,9 @@
             copy.wait()
         early[order[i]] = early[order[i]] + early_g[order[i]]
 
-    barrier = pltpu.get_barrier_semaphore()
-
-    def greet(d, carry):
-        pl.semaphore_signal(barrier, inc=1, device_id=plane(d)[1], device_id_type=MESH)
-        return carry
-
-    for d in (1, 2, 3):
-        pl.semaphore_signal(barrier, inc=1, device_id=to_y(lax.rem(y + d, 4)), device_id_type=MESH)
-    pl.semaphore_signal(barrier, inc=1, device_id=partner, device_id_type=MESH)
-    lax.fori_loop(0, 31, greet, 0)
-
     my_ranks = pl.ds(pl.multiple_of(64 * y, 64), 64)
-    load_r.wait()
-    rearly[my_ranks, :] = rown[:, pl.ds(pl.multiple_of(EARLY * x, EARLY), EARLY)]
-    rlate[my_ranks, :] = rown[:, EARLY_COLS:COLS]
+    rearly[my_ranks, :] = right_in[:, pl.ds(pl.multiple_of(EARLY * x, EARLY), EARLY)]
+    rlate[my_ranks, :] = right_in[:, EARLY_COLS:COLS]
     loaded(0)
     pl.semaphore_wait(barrier, 35)
 
@@ -522,7 +519,7 @@
             jax.ShapeDtypeStruct((8, ROWS), F32),
             jax.ShapeDtypeStruct((ROWS, COLS), F32),
         ),
-        in_specs=[pl.BlockSpec(memory_space=pltpu.HBM)] * 3,
+        in_specs=[pl.BlockSpec(memory_space=pltpu.HBM)] * 2 + [pl.BlockSpec(memory_space=pltpu.VMEM)],
         out_specs=(pl.BlockSpec(memory_space=pltpu.VMEM),) * 4,
         scratch_shapes=[
             vmem(4, ROWS, EARLY),
@@ -530,7 +527,6 @@
             vmem(ROWS, LATE_COLS),
             vmem(ROWS, LATE_COLS),
             vmem(4, ROWS, LATE),
-            vmem(64, COLS),
             vmem(ROWS, EARLY),
             vmem(ROWS, LATE_COLS),
             vmem(ROWS, CHUNK),
@@ -561,7 +557,7 @@
             vmem(16, 1, ROWS),
             pltpu.SemaphoreType.DMA((SENDS,)),
             pltpu.SemaphoreType.DMA((ARRIVALS,)),
-            pltpu.SemaphoreType.DMA((11,)),
+            pltpu.SemaphoreType.DMA((10,)),
             pltpu.SemaphoreType.DMA((6,)),
         ],
         compiler_params=pltpu.CompilerParams(
@@ -581,13 +577,12 @@
     sh, sl = split(ortho[...] * scale[0:1, :])
     column_ref[...] = jnp.broadcast_to(scale[0:1, :], (128, ROWS)).T
     column = column_ref[own, :]
-    column = jnp.concatenate([column] * (WIDTH // 128), axis=1)
-    for i in range(COLS // WIDTH):
-        cols = slice(WIDTH * i, WIDTH * (i + 1))
+    for i, (low, high) in enumerate(zip(EDGES[:-1], EDGES[1:])):
+        cols = slice(low, high)
         rh, rl = split(right[:, cols])
         normal = dot(sh, rh) + (dot(sh, rl) + dot(sl, rh))
         staged_w[:, cols] = weights[:, cols] - learning_rate * normal
-        staged_r[:, cols] = column * right[own, cols]
+        staged_r[:, cols] = jnp.concatenate([column] * ((high - low) // 128), axis=1) * right[own, cols]
         copies.append(pltpu.make_async_copy(staged_w.at[:, cols], new_weights.at[:, cols], sems.at[2 * i + 1]))
         copies[-1].start()
         copies.append(
@@ -598,7 +593,7 @@
         copy.wait()
 
 
-WIDTH = 1664
+EDGES = (0, 1280, 2304, 3072, 3328)
 
 
 def update(ortho, scale, right, weights, momentum):
@@ -615,7 +610,7 @@
             pltpu.VMEM((ROWS, COLS), F32),
             pltpu.VMEM((ROWS, 128), F32),
             pltpu.VMEM((64, COLS), F32),
-            pltpu.SemaphoreType.DMA((2 * (COLS // WIDTH) + 1,)),
+            pltpu.SemaphoreType.DMA((2 * len(EDGES) - 1,)),
         ],
         compiler_params=pltpu.CompilerParams(vmem_limit_bytes=40 * 1024 * 1024),
         name="update",

time: 96 us -> 95.8 us (level)
  no operation moved by 1% of the time
where the time goes in v5:
time: 95.8 us; the launch traced here: 95.6 us
  Pallas kernels  93.6 us (98%)
  local copies, waits for them, and re-layouts  1.15 us (1%)
    pallas_call x1, Pallas kernels, exchange(): pl.pallas_call(exchange_kernel, out_shape=(jax.ShapeDtypeStruct((ROWS, CO...  90.5 us
    pallas_call x1, Pallas kernels, update(): pl.pallas_call(update_kernel, out_shape=(jax.ShapeDtypeStruct((ROWS, COLS...  3.13 us

profile of v5, /device:TPU:1, one launch (start us, length us, event | category | flops | bytes accessed | tf_op | source)
XLA Modules:
  0.0 95.6 jit_solution(3076967794501574943)
XLA Ops:
  0.6 0.0 copy-start.1
  0.6 1.1 %copy-done.1 = f32[3328,64]{0,1:T(8,128)S(1)} copy-done((f32[3328,64]{0,1:T(8,128)S(1)}, f32[3328,64]{0,1:T(8,128)}, u32[]{:S(2)}) %copy-start.1) | copy-done | bytes 851992
  1.8 0.0 copy-start
  1.8 90.5 %exchange.1 = (f32[256,3328]{1,0:T(8,128)S(1)}, f32[256,256]{1,0:T(8,128)S(1)}, f32[8,256]{1,0:T(8,128)S(1)}, f32[256,3328]{1,0:T(8,128)S(1)}) custom-call(f32[256,3328]{1,0:T(8,128)} %momentum.1, f32[256,3328]{1,0:T(8,128)} %gradient.1, f32[64,3328]{1,0:T(8,128)S(1)} %bitcast.2), custom_call_target="tpu_custom_call" | custom-call | flops 1744830464 | bytes 11000000 | tf_op jit(solution)/shard_map/exchange/pallas_call | solution.py:514
  92.3 0.0 copy-done
  92.3 3.1 %update.1 = (f32[256,3328]{1,0:T(8,128)}, f32[256,3328]{1,0:T(8,128)}, f32[64,3328]{1,0:T(8,128)}) custom-call(f32[256,256]{1,0:T(8,128)S(1)} %get-tuple-element.10.ortho, f32[8,256]{1,0:T(8,128)S(1)} %get-tuple-element.11.scale, f32[256,3328]{1,0:T(8,128)S(1)} %get-tuple-element.12.right, f32[256,3328]{1,0:T(8,128)S(1)} %copy-done, ...), custom_call_target="tpu_custom_call" | custom-call | tf_op jit(solution)/shard_map/update/pallas_call | solution.py:600
Async XLA Ops:
  0.6 1.2 %copy-start.1 = (f32[3328,64]{0,1:T(8,128)S(1)}, f32[3328,64]{0,1:T(8,128)}, u32[]{:S(2)}) copy-start(f32[3328,64]{0,1:T(8,128)} %param.7) | copy-start | bytes 2555908
  1.8 90.5 %copy-start = (f32[256,3328]{1,0:T(8,128)S(1)}, f32[256,3328]{1,0:T(8,128)}, u32[]{:S(2)}) copy-start(f32[256,3328]{1,0:T(8,128)} %weights.1) | copy-start | bytes 10223620
